TPU v7x, 256 devices: a whole 4x4x8 slice. The times are simulated.
256 devices in a mesh: aa: 64 (over z, y, core), pb: 4 (over x).
Axes of the slice: x: 4, y: 4, z: 8, core: 2. Of those that a mesh axis runs over, the one named last changes fastest.
Arguments:
- wave_field: float32 [64, 2, 128, 512], P('aa'), may hold values from -6 to 6
- scaled_dual: float32 [64, 2, 128, 512], P('aa', None, None, 'pb'), may hold values from -4 to 4
- intensity: float32 [64, 64, 4096], P('aa', 'pb'), may hold values from 0 to 2
- probe_field: float32 [2, 64, 64], replicated, may hold values from -5 to 5
- scan_rows: int32 [64, 64], P('aa', 'pb'), may hold values from 0 to 64
- scan_cols: int32 [64, 64], P('aa', 'pb'), may hold values from 0 to 448
- sample_mask: int32 [64, 64], P('aa', 'pb'), may hold values 0 or 1
- object_field: float32 [2, 128, 512, 512], P(None, 'aa', 'pb'), may hold values from -6 to 6
- ray_blocks: int32 [64, 8, 12], replicated, may hold values from 0 to 63
- ray_tables: int32 [64, 8, 12], replicated, may hold values from 0 to 11
- radon_weights: bfloat16 [4096, 768], replicated, may hold values from -0.02734375 to 0.02734375
Outputs:
- wave_next: float32 [64, 2, 128, 512], P('aa', None, None, 'pb')
- probe_next: float32 [2, 64, 64], replicated
- object_next: float32 [2, 128, 512, 512], P(None, 'aa', 'pb')
Inputs may be any that keep to these rules, and one draw needn't show every extreme that they name: `scan_rows`: each scan window lies inside the projection. `scan_cols`: each scan window lies inside the projection. `ray_blocks`: a block may appear several times in one list.
All inputs are finite; a program needn't handle non-finite values. No bound on the sum of `sample_mask` on one device may be relied on, other than what follows from the above.
Results may differ from a plain program's by a relative error of at most 0.00065.
The roundings to bfloat16 on the way count: a program that leaves them out, or rounds other values in their place, can miss the bound.
Values may be sent and summed in bfloat16 or wider, within the bound.
A program may use at most 128 MiB of HBM per device.

v0:
```python
import math

import jax
import jax.numpy as jnp
from jax import lax
from jax.sharding import PartitionSpec as P

BLK = 64
NW = 12
NB = 8
BLOCKS = 64
BIN = 64
PIXB = 4096


WAVE_STEP = 0.05
PENALTY = 1.0
PROBE_STEP = 0.05
OBJECT_STEP = 1.0


def dft_tables(size):
    index = jnp.arange(size, dtype=jnp.int32)
    phase = index[:, None] * index[None, :] % size
    angle = phase.astype(jnp.float32) * (-2.0 * math.pi / size)
    scale = 1.0 / math.sqrt(size)
    return (jnp.cos(angle) * scale, jnp.sin(angle) * scale)


def transform(field_re, field_im, tab_re, tab_im):
    highest = lax.Precision.HIGHEST

    def apply_left(table, field):
        return jnp.einsum("ik,nkl->nil", table, field, precision=highest)

    def apply_right(field, table):
        return jnp.einsum("nil,lj->nij", field, table, precision=highest)

    half_re = apply_left(tab_re, field_re) - apply_left(tab_im, field_im)
    half_im = apply_left(tab_re, field_im) + apply_left(tab_im, field_re)
    out_re = apply_right(half_re, tab_re) - apply_right(half_im, tab_im)
    out_im = apply_right(half_re, tab_im) + apply_right(half_im, tab_re)
    return (out_re, out_im)


def ptycho_grads(waves, probe, scan_rows, scan_cols, sample_mask, intensity):
    count_ang, count_pos = scan_rows.shape
    size = probe.shape[-1]
    angle_col = jnp.broadcast_to(
        jnp.arange(count_ang, dtype=jnp.int32)[:, None], (count_ang, count_pos)
    )
    starts = jnp.stack([angle_col, scan_rows, scan_cols], axis=-1).reshape(-1, 3)
    zero_index = jnp.zeros((), jnp.int32)

    def cut_window(start):
        piece = lax.dynamic_slice(
            waves, (start[0], zero_index, start[1], start[2]), (1, 2, size, size)
        )
        return piece[0]

    windows = jax.vmap(cut_window)(starts)
    win_re = windows[:, 0]
    win_im = windows[:, 1]
    probe_re = probe[0]
    probe_im = probe[1]
    patch_re = probe_re * win_re - probe_im * win_im
    patch_im = probe_re * win_im + probe_im * win_re
    tab_re, tab_im = dft_tables(size)
    far_re, far_im = transform(patch_re, patch_im, tab_re, tab_im)
    live = sample_mask.reshape(-1, 1, 1).astype(jnp.float32)
    factor = live * (far_re * far_re + far_im * far_im - intensity.reshape(-1, size, size))
    back_re, back_im = transform(factor * far_re, factor * far_im, tab_re, -tab_im)
    grad_re = probe_re * back_re + probe_im * back_im
    grad_im = probe_re * back_im - probe_im * back_re
    updates = jnp.stack([grad_re, grad_im], axis=1)
    numbers = lax.ScatterDimensionNumbers(
        update_window_dims=(1, 2, 3),
        inserted_window_dims=(0,),
        scatter_dims_to_operand_dims=(0, 2, 3),
    )
    wave_grad = lax.scatter_add(jnp.zeros(waves.shape, jnp.float32), starts, updates, numbers)
    probe_re_grad = jnp.sum(win_re * back_re + win_im * back_im, axis=0)
    probe_im_grad = jnp.sum(win_re * back_im - win_im * back_re, axis=0)
    return (wave_grad, jnp.stack([probe_re_grad, probe_im_grad]))


def ray_onehot(ray_blocks, ray_tables):
    keys = ray_blocks * NW + ray_tables
    columns = jnp.arange(BLOCKS * NW, dtype=jnp.int32)
    hits = jnp.zeros(keys.shape[:2] + (BLOCKS * NW,), jnp.float32)
    for entry in range(keys.shape[2]):
        hits = hits + (keys[:, :, entry, None] == columns).astype(jnp.float32)
    return hits.astype(jnp.bfloat16)


def shards(
    wave_field,
    scaled_dual,
    intensity,
    probe_field,
    scan_rows,
    scan_cols,
    sample_mask,
    object_field,
    ray_blocks,
    ray_tables,
    radon_weights,
):
    ranks = lax.axis_size("pb")
    column = lax.axis_index("pb")
    depth = object_field.shape[1]
    slab_cols = object_field.shape[2]
    width = object_field.shape[3]
    block_rows = slab_cols // BLK
    own_cols = block_rows * NB * NW
    angles = ray_blocks.shape[0]
    hits = ray_onehot(ray_blocks, ray_tables)
    col_hits = lax.dynamic_slice_in_dim(
        hits.reshape(angles * NB, BLOCKS * NW), column * own_cols, own_cols, 1
    )
    object_bf = object_field.astype(jnp.bfloat16)
    whole = lax.all_gather(object_bf, "pb", axis=2, tiled=True)
    tiles = whole.reshape(2, depth, NB, BLK, NB, BLK).transpose(0, 1, 2, 4, 3, 5).reshape(-1, PIXB)
    products = jnp.dot(tiles, radon_weights, preferred_element_type=jnp.float32).astype(
        jnp.bfloat16
    )
    stacked = (
        products.reshape(2, depth, BLOCKS, NW, BIN)
        .transpose(2, 3, 0, 1, 4)
        .reshape(BLOCKS * NW, 2 * depth * BIN)
    )
    row_hits = lax.dynamic_slice_in_dim(hits, column * block_rows, block_rows, 1).reshape(
        angles * block_rows, BLOCKS * NW
    )
    projection = jnp.dot(row_hits, stacked, preferred_element_type=jnp.float32)
    projection = (
        projection.reshape(angles, block_rows, 2, depth, BIN)
        .transpose(0, 2, 3, 1, 4)
        .reshape(angles, 2, depth, slab_cols)
    )
    angle_proj = lax.all_to_all(projection, "aa", split_axis=0, concat_axis=2, tiled=True)
    wave_grad, probe_grad = ptycho_grads(
        wave_field, probe_field, scan_rows, scan_cols, sample_mask, intensity
    )
    wave_share = lax.psum_scatter(wave_grad, "pb", scatter_dimension=3, tiled=True)
    probe_total = lax.psum(probe_grad, ("aa", "pb"))
    positions = scan_rows.shape[1] * ranks
    probe_next = probe_field - PROBE_STEP / (angles * positions) * probe_total
    wave_own = lax.dynamic_slice_in_dim(wave_field, column * slab_cols, slab_cols, 3)
    wave_next = wave_own - WAVE_STEP * (
        wave_share + PENALTY * (wave_own - angle_proj + scaled_dual)
    )
    target = wave_next + scaled_dual
    slab_target = lax.all_to_all(target, "aa", split_axis=2, concat_axis=0, tiled=True)
    misfit = (projection - slab_target).astype(jnp.bfloat16)
    full_misfit = lax.all_gather(misfit, "pb", axis=3, tiled=True)
    rays = (
        full_misfit.reshape(angles, 2, depth, NB, BIN)
        .transpose(0, 3, 1, 2, 4)
        .reshape(angles * NB, 2 * depth * BIN)
    )
    table_sums = lax.dot_general(
        col_hits, rays, (((0,), (0,)), ((), ())), preferred_element_type=jnp.float32
    ).astype(jnp.bfloat16)
    spread = (
        table_sums.reshape(block_rows * NB, NW, 2, depth, BIN)
        .transpose(2, 3, 0, 1, 4)
        .reshape(2 * depth * block_rows * NB, NW * BIN)
    )
    object_grad = lax.dot_general(
        spread, radon_weights, (((1,), (1,)), ((), ())), preferred_element_type=jnp.float32
    )
    object_grad = (
        object_grad.reshape(2, depth, block_rows, NB, BLK, BLK)
        .transpose(0, 1, 2, 4, 3, 5)
        .reshape(2, depth, slab_cols, width)
    )
    object_next = object_field - OBJECT_STEP * object_grad
    return (wave_next, probe_next, object_next)


def solution(mesh):
    return jax.shard_map(
        shards,
        mesh=mesh,
        in_specs=(
            P("aa", None, None, None),
            P("aa", None, None, "pb"),
            P("aa", "pb", None),
            P(),
            P("aa", "pb"),
            P("aa", "pb"),
            P("aa", "pb"),
            P(None, "aa", "pb", None),
            P(),
            P(),
            P(),
        ),
        out_specs=(P("aa", None, None, "pb"), P(), P(None, "aa", "pb", None)),
        check_vma=False,
    )
```

profile of v0, /device:TPU:1, one launch (start us, length us, event | category | flops | bytes accessed | tf_op | source)
XLA Modules:
  0.0 381.5 jit_solution(17286622461515735002)
XLA Ops:
  7.2 2.1 convert_element_type.150
  9.5 45.0 %while.2 = (s32[]{:T(128)}, f32[1,2,128,512]{3,2,1,0:T(8,128)}, s32[16,4]{0,1:T(4,128)S(1)}, f32[16,1,2,64,64]{4,3,0,2,1:T(8,128)S(1)}, s32[]{:T(128)}) while((s32[]{:T(128)}, f32[1,2,128,512]{3,2,1,0:T(8,128)}, s32[16,4]{0,1:T(4,128)S(1)}, f32[16,1,2,64,64]{4,3,0,2,1:T(8,128)S(1)}, s32[]{:T(128)}) %tuple.76), condition=%wide.while_cond, body=%wide.while_body.sunk | while | flops 2 | bytes 98437 | solution.py:56
  10.1 2.2 bitcast_dynamic-update-slice_fusion.2
  12.9 2.2 bitcast_dynamic-update-slice_fusion.2
  15.7 2.2 bitcast_dynamic-update-slice_fusion.2
  18.6 2.2 bitcast_dynamic-update-slice_fusion.2
  21.4 2.2 bitcast_dynamic-update-slice_fusion.2
  24.2 2.2 bitcast_dynamic-update-slice_fusion.2
  27.0 2.2 bitcast_dynamic-update-slice_fusion.2
  29.8 2.2 bitcast_dynamic-update-slice_fusion.2
  32.6 2.2 bitcast_dynamic-update-slice_fusion.2
  35.4 2.2 bitcast_dynamic-update-slice_fusion.2
  38.2 2.2 bitcast_dynamic-update-slice_fusion.2
  41.1 2.2 bitcast_dynamic-update-slice_fusion.2
  43.9 2.2 bitcast_dynamic-update-slice_fusion.2
  46.7 2.2 bitcast_dynamic-update-slice_fusion.2
  49.5 2.2 bitcast_dynamic-update-slice_fusion.2
  52.3 2.2 bitcast_dynamic-update-slice_fusion.2
  72.4 127.0 %while.3 = (s32[]{:T(128)}, f32[1,2,128,512]{3,2,1,0:T(8,128)S(1)}, s32[16,3]{0,1:T(4,128)S(1)}, f32[16,2,64,64]{3,2,0,1:T(8,128)S(1)}, s32[]{:T(128)}, /*index=5*/s32[4]{0:T(128)S(1)}, s32[1]{0:T(128)}, s32[]{:T(128)}) while((s32[]{:T(128)}, f32[1,2,128,512]{3,2,1,0:T(8,128)S(1)}, s32[16,3]{0,1:T(4,128)S(1)}, f32[16,2,64,64]{3,2,0,1:T(8,128)S(1)}, ...), condition=%wide.while_cond.1, body=%wide.while_body.1.sunk | while | flops 16413 | bytes 164035 | solution.py:81
  73.0 2.6 and_reduce_fusion.2
  77.5 2.6 dynamic-update-slice.8
  80.7 2.6 and_reduce_fusion.2
  85.2 2.9 dynamic-update-slice.8
  88.7 2.6 and_reduce_fusion.2
  93.2 2.9 dynamic-update-slice.8
  96.7 2.6 and_reduce_fusion.2
  101.2 2.9 dynamic-update-slice.8
  104.7 2.6 and_reduce_fusion.2
  109.2 2.9 dynamic-update-slice.8
  112.8 2.6 and_reduce_fusion.2
  117.3 2.9 dynamic-update-slice.8
  120.8 2.6 and_reduce_fusion.2
  127.9 2.6 and_reduce_fusion.2
  132.4 2.8 dynamic-update-slice.8
  135.9 2.6 and_reduce_fusion.2
  140.4 2.8 dynamic-update-slice.8
  143.8 2.6 and_reduce_fusion.2
  148.3 2.9 dynamic-update-slice.8
  151.9 2.6 and_reduce_fusion.2
  156.4 2.8 dynamic-update-slice.8
  159.8 2.6 and_reduce_fusion.2
  164.3 2.8 dynamic-update-slice.8
  167.7 2.6 and_reduce_fusion.2
  172.2 3.0 dynamic-update-slice.8
  175.8 2.6 and_reduce_fusion.2
  180.3 3.0 dynamic-update-slice.8
  183.9 2.6 and_reduce_fusion.2
  188.4 2.9 dynamic-update-slice.8
  191.9 2.6 and_reduce_fusion.2
  196.4 3.0 dynamic-update-slice.8
  200.3 83.1 %psum.7 = f32[2,64,64]{2,1,0:T(8,128)S(1)} all-reduce(f32[2,64,64]{2,1,0:T(8,128)S(1)} %pad_maximum_fusion.1), channel_id=1, replica_groups=mesh['aa'=64,'pb'=4] {'aa','pb'}, use_global_device_ids=true, to_apply=%region_4.5 | all-reduce | flops 8192 | bytes 65536 | tf_op jit(solution)/shard_map/psum | solution.py:146
  287.8 2.1 convert_add_fusion.1
  290.0 6.2 %reshape.85 = bf16[2,2,8,64,8,64]{5,4,3,2,1,0:T(8,128)(2,1)} reshape(bf16[2,2,512,512]{3,2,1,0:T(8,128)(2,1)} %all-gather.2.cloned.1.call-done) | data formatting | bytes 4194304 | tf_op jit(solution)/shard_map/reshape | solution.py:123
  296.1 5.4 %copy.181 = bf16[2,2,8,64,8,64]{5,3,4,2,1,0:T(8,128)(2,1)} copy(bf16[2,2,8,64,8,64]{5,4,3,2,1,0:T(8,128)(2,1)} %reshape.85) | data formatting | bytes 4194304 | tf_op jit(solution)/shard_map/reshape | solution.py:123
  301.5 5.7 %reshape.86 = bf16[256,4096]{1,0:T(8,128)(2,1)S(1)} reshape(bf16[2,2,8,8,64,64]{5,4,3,2,1,0:T(8,128)(2,1)} %bitcast.245) | data formatting | bytes 4194304 | tf_op jit(solution)/shard_map/reshape | solution.py:123
  307.2 4.6 %convolution_convert_fusion = bf16[256,768]{1,0:T(8,128)(2,1)S(1)} fusion(bf16[256,4096]{1,0:T(8,128)(2,1)S(1)} %reshape.86, bf16[4096,768]{1,0:T(8,128)(2,1)} %param.21), kind=kOutput, calls=%fused_computation.29 | convolution fusion | flops 1610809344 | bytes 8781824 | tf_op jit(solution)/shard_map/dot_general | solution.py:124
  316.4 5.7 %all-to-all-start = ((f32[64,2,2,128]{3,2,1,0:T(2,128)}), f32[64,2,2,128]{3,2,1,0:T(2,128)S(1)}, u32[]{:S(2)}, u32[]{:S(2)}) async-start(f32[64,2,2,128]{3,2,1,0:T(2,128)} %copy.132), calls=%async_computation.1 | async-start | bytes 262144 | tf_op jit(solution)/shard_map/all_to_all | solution.py:141
  323.7 9.6 %all-to-all-done = f32[64,2,2,128]{3,2,1,0:T(2,128)S(1)} async-done(((f32[64,2,2,128]{3,2,1,0:T(2,128)}), f32[64,2,2,128]{3,2,1,0:T(2,128)S(1)}, u32[]{:S(2)}, u32[]{:S(2)}) %all-to-all-start) | async-done | bytes 131104 | tf_op jit(solution)/shard_map/all_to_all | solution.py:141
  335.7 4.4 %all-to-all-start.1 = ((f32[1,2,128,128]{3,1,0,2:T(2,128)}), f32[1,2,128,128]{3,1,0,2:T(2,128)S(1)}, u32[]{:S(2)}, u32[]{:S(2)}) async-start(f32[1,2,128,128]{3,1,0,2:T(2,128)} %copy.146), calls=%async_computation.2 | async-start | bytes 262144 | tf_op jit(solution)/shard_map/all_to_all | solution.py:154
  341.3 10.2 %all-to-all-done.1 = f32[1,2,128,128]{3,1,0,2:T(2,128)S(1)} async-done(((f32[1,2,128,128]{3,1,0,2:T(2,128)}), f32[1,2,128,128]{3,1,0,2:T(2,128)S(1)}, u32[]{:S(2)}, u32[]{:S(2)}) %all-to-all-start.1) | async-done | bytes 131104 | tf_op jit(solution)/shard_map/all_to_all | solution.py:154
  351.6 9.0 %all_gather.7 = bf16[64,2,2,512]{3,0,2,1:T(8,128)(2,1)S(1)} all-gather(bf16[64,2,2,128]{3,0,2,1:T(8,128)(2,1)S(1)} %fusion.24), channel_id=1, replica_groups=mesh['aa'=64,'pb'=4] {'pb'}, dimensions={3}, use_global_device_ids=true | all-gather | bytes 327680 | tf_op jit(solution)/shard_map/all_gather | solution.py:156
  361.8 2.0 convolution_convert_fusion.1
  364.2 7.2 %convolution_bitcast_fusion = f32[2,2,2,64,8,64]{5,4,3,2,1,0:T(8,128)} fusion(bf16[64,64,768,1,1,1]{2,1,0,5,4,3:T(8,128)(2,1)} %bitcast.263, bf16[2,2,2,8,768,1]{4,3,2,1,0,5:T(8,128)(2,1)S(1)} %reshape.158), kind=kOutput, calls=%fused_computation.6 | convolution fusion | flops 402653184 | bytes 7438336 | tf_op jit(solution)/shard_map/dot_general | solution.py:170
  371.4 2.0 reshape.93
  (190 shorter events, 87.2 us)
Async XLA Ops:
  7.2 2.3 copy-start.8
  7.2 2.3 copy-start.9
  7.2 47.3 %copy-start.3 = (f32[2,64,64]{2,1,0:T(8,128)S(1)}, f32[2,64,64]{2,1,0:T(8,128)}, u32[]{:S(2)}) copy-start(f32[2,64,64]{2,1,0:T(8,128)} %param.14) | copy-start | bytes 98308
  7.2 282.8 %all-gather.2.cloned.1.call-start = ((), (), s32[]{:S(2)}) async-start(), calls=%async_computation.4 | async-start | bytes 2621440 | tf_op jit(solution)/shard_map/all_gather | solution.py:122
  9.4 324.0 %reduce-scatter.2.cloned.1.call-start = ((), (), s32[]{:S(2)}) async-start(), calls=%async_computation.3 | async-start | bytes 655360 | tf_op jit(solution)/shard_map/reduce_scatter | solution.py:145
  56.7 3.2 copy-start.2
  58.8 2.4 copy-start.10
  71.7 0.7 copy-start.7
  71.8 128.4 %copy-start.5 = (s32[64,8,12]{0,1,2:T(8,128)S(1)}, s32[64,8,12]{0,1,2:T(8,128)}, u32[]{:S(2)}) copy-start(s32[64,8,12]{0,1,2:T(8,128)} %param.20) | copy-start | bytes 73732
  71.8 128.4 %copy-start.6 = (s32[64,8,12]{0,1,2:T(8,128)S(1)}, s32[64,8,12]{0,1,2:T(8,128)}, u32[]{:S(2)}) copy-start(s32[64,8,12]{0,1,2:T(8,128)} %param.19) | copy-start | bytes 73732
  199.4 0.8 copy-start.1
  315.4 17.9 %copy-start.4 = (f32[1,2,128,128]{3,2,1,0:T(8,128)S(1)}, f32[1,2,128,128]{3,2,1,0:T(8,128)}, u32[]{:S(2)}) copy-start(f32[1,2,128,128]{3,2,1,0:T(8,128)} %param.12) | copy-start | bytes 393220
  316.4 16.8 %all-to-all-start = ((f32[64,2,2,128]{3,2,1,0:T(2,128)}), f32[64,2,2,128]{3,2,1,0:T(2,128)S(1)}, u32[]{:S(2)}, u32[]{:S(2)}) async-start(f32[64,2,2,128]{3,2,1,0:T(2,128)} %copy.132), calls=%async_computation.1 | async-start | bytes 262144 | tf_op jit(solution)/shard_map/all_to_all | solution.py:141
  335.7 15.8 %all-to-all-start.1 = ((f32[1,2,128,128]{3,1,0,2:T(2,128)}), f32[1,2,128,128]{3,1,0,2:T(2,128)S(1)}, u32[]{:S(2)}, u32[]{:S(2)}) async-start(f32[1,2,128,128]{3,1,0,2:T(2,128)} %copy.146), calls=%async_computation.2 | async-start | bytes 262144 | tf_op jit(solution)/shard_map/all_to_all | solution.py:154
  371.4 2.0 copy-start
Sparse Core Ops, SparseCore 0:
  9.8 37.1 all-gather.1
  200.3 27.2 reduce-scatter.1
where the time goes:
time: 385 us; the launch traced here: 381 us
  local copies, waits for them, and re-layouts  128 us (33%)
  blocking collectives  92.2 us (24%)
  other arithmetic  84.1 us (22%)
  matrix products  32.1 us (8%)
  waiting for transfers between devices  19.9 us (5%)
  between operations  14.6 us (4%)
  starting transfers between devices  10.2 us (3%)
    psum x1, blocking collectives, shards(): probe_total = lax.psum(probe_grad, ('aa', 'pb'))  83.1 us
    scatter-add x32, other arithmetic  71.9 us
    scatter-add x48, local copies, waits for them, and re-layouts  54.7 us
    gather x48, local copies, waits for them, and re-layouts  44.9 us
    reshape x3, local copies, waits for them, and re-layouts, shards(): whole.reshape(2, depth, NB, BLK, NB, BLK).transpose(0, 1, 2, 4, 3, 5)  17.2 us
    all_to_all x1, waiting for transfers between devices, shards(): lax.all_to_all(target, 'aa', split_axis=2, concat_axis=0, tiled=True)  10.2 us
    all_to_all x1, waiting for transfers between devices, shards(): lax.all_to_all(projection, 'aa', split_axis=0, concat_axis=2, tiled=True)  9.56 us
    all_gather x1, blocking collectives, shards(): full_misfit = lax.all_gather(misfit, 'pb', axis=3, tiled=True)  9.04 us
  transfers between devices with their start and end apart: 4, of which 2 were waited for; matrix products, arithmetic and copies ran while one was open for 59% of the time, Pallas kernels for 0%

commit v1 on v0

v1 whole, which is shorter than its diff:
```python
import math

import jax
import jax.numpy as jnp
import ml_dtypes
import numpy as np
from jax import lax
from jax.experimental import pallas as pl
from jax.experimental.pallas import tpu as pltpu
from jax.sharding import PartitionSpec as P

BLK = 64
NW = 12
NB = 8
LIST = 12
AA = 64
PB = 4
ZC = 4
POS = 16
PAIRS = 8
KEYS = 192
MESH_Y_CORE = 8
SLOT = 8
WCH = 8
WROWS = 4096 // WCH

WAVE_STEP = 0.05
PENALTY = 1.0
PROBE_STEP = 0.05
OBJECT_STEP = 1.0

F32 = jnp.float32
BF16 = jnp.bfloat16


def split_np(table):
    high = table.astype(ml_dtypes.bfloat16)
    low = (table - high.astype(np.float64)).astype(ml_dtypes.bfloat16)
    return high, low


def dft_constants():
    index = np.arange(BLK)
    phase = (index[:, None] * index[None, :]) % BLK
    angle = phase.astype(np.float64) * (-2.0 * math.pi / BLK)
    f_re, f_im = np.cos(angle) / math.sqrt(BLK), np.sin(angle) / math.sqrt(BLK)
    pair = np.eye(2)

    def right(re, im):
        dre, dim = np.kron(pair, re), np.kron(pair, im)
        return np.block([[dre, dim], [-dim, dre]])

    def left(re, im):
        high, low = split_np(np.block([[re, -im], [im, re]]))
        return np.concatenate(
            [np.concatenate([high, high], 1), np.concatenate([low, low], 1)], 0
        )

    order = np.concatenate([np.arange(0, BLK, 2), np.arange(1, BLK, 2)])
    g_hi, g_lo = split_np(right(f_re, f_im))
    b_hi, b_lo = split_np(right(f_re, -f_im))
    l_fwd = left(f_re[order, :], f_im[order, :])
    l_bwd = left(f_re[:, order], -f_im[:, order])
    return np.stack([g_hi, g_lo, b_hi, b_lo, l_fwd, l_bwd])


def halves(value):
    high = value.astype(BF16)
    low = (value - high.astype(F32)).astype(BF16)
    return high, low


def dot(lhs, rhs):
    return jnp.dot(lhs, rhs, preferred_element_type=F32)


def right_apply(re, im, g_hi, g_lo):
    high, low = halves(jnp.concatenate([re, im], axis=1))
    out = dot(high, g_hi) + dot(low, g_hi) + dot(high, g_lo)
    return out[:, :128], out[:, 128:]


def left_apply(re, im, table):
    high, low = halves(jnp.concatenate([re, im], axis=0))
    out = dot(table, jnp.concatenate([high, low], axis=0))
    out = out[:128] + out[128:]
    return out[:64], out[64:]


def rows_to_lanes(value):
    return jnp.concatenate([value[q * 64 : (q + 1) * 64] for q in range(PAIRS)], axis=1)


def lanes_to_rows(value):
    return jnp.concatenate([value[:, q * 128 : (q + 1) * 128] for q in range(PAIRS)], axis=0)


def swap(value):
    return pltpu.roll(value, 64, 1)


def interleave(first, second):
    low = lax.broadcasted_iota(jnp.int32, first.shape, 1) < 64
    return jnp.where(low, first, swap(second)), jnp.where(low, swap(first), second)


def kernel(
    rows_ref,
    cols_ref,
    mask_ref,
    obj_hbm,
    wts_hbm,
    wave_hbm,
    dual_hbm,
    int_hbm,
    probe_hbm,
    tab_hbm,
    rowkey_hbm,
    colkey_hbm,
    wave_out,
    probe_out,
    obj_out,
    obj,
    wts,
    wave,
    dual,
    inten,
    probe,
    tab,
    rowkey,
    colkey,
    lhs,
    ptile,
    stk,
    hit_r,
    hit_c,
    win_r,
    win_i,
    gra_r,
    gra_i,
    pad,
    acc,
    share,
    base,
    send1,
    recv1,
    send2,
    recv2,
    wnext,
    rays,
    spread,
    onew,
    prow,
    pfull,
    pout,
    in_sem,
    w_sem,
    out_sem,
    x_send,
    x_recv,
    a_send,
    a_recv,
):
    me_a = lax.axis_index("aa")
    me_p = lax.axis_index("pb")
    z_base = (me_a // MESH_Y_CORE) * MESH_Y_CORE
    z_own = me_a // MESH_Y_CORE
    m_own = me_a % MESH_Y_CORE

    def lanes(shape):
        return lax.broadcasted_iota(jnp.int32, shape, 1)

    obj_in = [
        pltpu.make_async_copy(
            obj_hbm.at[:, pl.ds(t * 128, 128)], obj.at[pl.ds(t * 512, 512)], in_sem.at[t]
        )
        for t in range(4)
    ]
    wts_in = [
        pltpu.make_async_copy(
            wts_hbm.at[pl.ds(c * WROWS, WROWS)], wts.at[pl.ds(c * WROWS, WROWS)], w_sem.at[c]
        )
        for c in range(WCH)
    ]
    wave_in = [
        pltpu.make_async_copy(
            wave_hbm.at[:, pl.ds(t * 128, 128)], wave.at[pl.ds(t * 256, 256)], in_sem.at[4 + t]
        )
        for t in range(4)
    ]
    others = {
        name: pltpu.make_async_copy(src, dst, in_sem.at[8 + n])
        for n, (name, src, dst) in enumerate(
            [
                ("rowkey", rowkey_hbm, rowkey),
                ("colkey", colkey_hbm, colkey),
                ("probe", probe_hbm, probe),
                ("tab", tab_hbm, tab),
                ("inten", int_hbm, inten),
                ("dual", dual_hbm, dual),
            ]
        )
    }
    others["rowkey"].start()
    for copy in obj_in + wts_in + wave_in:
        copy.start()
    for name in ("probe", "tab", "inten", "dual", "colkey"):
        others[name].start()

    barrier = pltpu.get_barrier_semaphore()

    def greet(step, carry):
        peer = lax.rem(me_a + step, AA)
        pl.semaphore_signal(
            barrier, inc=1, device_id={"aa": peer}, device_id_type=pl.DeviceIdType.MESH
        )
        return carry

    lax.fori_loop(1, AA, greet, 0)
    for step in range(1, PB):
        pl.semaphore_signal(
            barrier,
            inc=1,
            device_id={"pb": lax.rem(me_p + step, PB)},
            device_id_type=pl.DeviceIdType.MESH,
        )

    others["rowkey"].wait()
    keys = rowkey[...]
    for t in range(6):
        column = lanes((128, 128)) + t * 128
        total = jnp.zeros((128, 128), F32)
        for e in range(LIST):
            total = total + jnp.where(keys[:, e : e + 1] == column, 1.0, 0.0)
        hit_r[:, t * 128 : (t + 1) * 128] = total.astype(BF16)

    for copy in obj_in:
        copy.wait()

    def fold(q, carry):
        for t in range(4):
            even = obj[pl.ds(t * 512 + 2 * q, 8, stride=64), :]
            odd = obj[pl.ds(t * 512 + 2 * q + 1, 8, stride=64), :]
            first, second = interleave(even, odd)
            at = pl.multiple_of(q * 64 + t * 16, 16)
            lhs[pl.ds(at, 16), :] = jnp.concatenate([first, second], axis=0)
        return carry

    lax.fori_loop(0, 32, fold, 0, unroll=4)
    products = jnp.zeros((64, 768), F32)
    per = 32 // WCH
    for c in range(WCH):
        wts_in[c].wait()
        part = jnp.concatenate(
            [lhs[(c * per + n) * 64 : (c * per + n + 1) * 64, :] for n in range(per)], axis=1
        ).astype(BF16)
        products = products + dot(part, wts[c * WROWS : (c + 1) * WROWS, :])
    for t in range(6):
        ptile[t * 64 : (t + 1) * 64, :] = products[:, t * 128 : (t + 1) * 128]
    own_stk = pl.multiple_of(me_p * KEYS, KEYS)
    for t in range(6):
        lists = [[], []], [[], []]
        for br in range(2):
            part = [ptile[pl.ds(t * 64 + cz * 2 + br, 8, stride=8), :] for cz in range(ZC)]
            for c in range(2):
                even, odd = interleave(part[2 * c], part[2 * c + 1])
                lists[0][c].append(even)
                lists[1][c].append(odd)
        for h in range(2):
            for c in range(2):
                stk[
                    pl.ds(pl.multiple_of(own_stk + (2 * t + h) * 16, 16), 16),
                    c * 128 : (c + 1) * 128,
                ] = jnp.concatenate(lists[h][c], axis=0).astype(BF16)

    pl.semaphore_wait(barrier, AA - 1 + PB - 1)

    def to_x(stage, step, src, dst):
        peer = lax.rem(me_p + step, PB)
        return pltpu.make_async_remote_copy(
            src_ref=src,
            dst_ref=dst,
            send_sem=x_send.at[stage * 3 + step - 1],
            recv_sem=x_recv.at[stage * 3 + step - 1],
            device_id={"pb": peer},
            device_id_type=pl.DeviceIdType.MESH,
        )

    own_block = stk.at[pl.ds(own_stk, KEYS)]
    gathers = [to_x(0, step, own_block, own_block) for step in range(1, PB)]
    for copy in gathers:
        copy.start()

    for copy in wave_in:
        copy.wait()

    def windows(q, carry):
        at = pl.multiple_of(q * 64, 64)
        for c, ref in ((0, win_r), (1, win_i)):
            found = []
            for h in range(2):
                row = rows_ref[0, 2 * q + h]
                col = cols_ref[0, 2 * q + h]
                tile = col // 128
                off = col % 128
                near = wave[pl.ds(tile * 256 + c * 128 + row, 64), :]
                far = wave[pl.ds(jnp.minimum(tile + 1, 3) * 256 + c * 128 + row, 64), :]
                both = jnp.where(lanes((64, 128)) >= off, near, far)
                found.append(pltpu.roll(both, (128 + 64 * h - off) % 128, 1))
            ref[pl.ds(at, 64), :] = jnp.where(lanes((64, 128)) < 64, found[0], found[1])
        return carry

    lax.fori_loop(0, PAIRS, windows, 0)
    others["probe"].wait()
    others["tab"].wait()
    others["inten"].wait()
    p_re = jnp.concatenate([probe[0]] * PAIRS, axis=0)
    p_im = jnp.concatenate([probe[1]] * PAIRS, axis=0)
    w_re, w_im = win_r[...], win_i[...]
    half_re, half_im = right_apply(
        p_re * w_re - p_im * w_im, p_re * w_im + p_im * w_re, tab[0], tab[1]
    )
    far_re, far_im = left_apply(rows_to_lanes(half_re), rows_to_lanes(half_im), tab[4])
    measured, live = [], []
    for q in range(PAIRS):
        even, odd = interleave(inten[2 * q], inten[2 * q + 1])
        measured.append(jnp.concatenate([even, odd], axis=0))
        live.append(
            jnp.where(
                lanes((1, 128)) < 64, mask_ref[0, 2 * q].astype(F32), mask_ref[0, 2 * q + 1].astype(F32)
            )
        )
    measured = jnp.concatenate(measured, axis=1)
    live = jnp.concatenate(live, axis=1)
    factor = live * (far_re * far_re + far_im * far_im - measured)
    half_re, half_im = left_apply(factor * far_re, factor * far_im, tab[5])
    back_re, back_im = right_apply(lanes_to_rows(half_re), lanes_to_rows(half_im), tab[2], tab[3])
    gra_r[...] = p_re * back_re + p_im * back_im
    gra_i[...] = p_re * back_im - p_im * back_re
    grad_re = jnp.sum((w_re * back_re + w_im * back_im).reshape(PAIRS, 64, 128), axis=0)
    grad_im = jnp.sum((w_re * back_im - w_im * back_re).reshape(PAIRS, 64, 128), axis=0)
    grad_re = grad_re + swap(grad_re)
    grad_im = grad_im + swap(grad_im)
    send1[pl.ds(4, 64, stride=SLOT), :] = jnp.where(lanes((64, 128)) < 64, grad_re, grad_im)

    pad[...] = jnp.zeros_like(pad)
    acc[...] = jnp.zeros_like(acc)

    def scatter(q, carry):
        at = pl.multiple_of(q * 64, 64)
        for h in range(2):
            row = rows_ref[0, 2 * q + h]
            col = cols_ref[0, 2 * q + h]
            turn = (col + 128 - 64 * h) % 128
            for c, ref in ((0, gra_r), (1, gra_i)):
                slot = (2 * h + c) * 192
                pad[slot + 64 : slot + 128, :] = pltpu.roll(ref[pl.ds(at, 64), :], turn, 1)
                moved = pad[pl.ds(slot + 64 - row, 128), :]
                for t in range(4):
                    place = lanes((128, 128)) + (t * 128 - col)
                    start = t * 256 + c * 128
                    acc[start : start + 128, :] = acc[start : start + 128, :] + jnp.where(
                        (place >= 0) & (place < 64), moved, 0.0
                    )
        return carry

    lax.fori_loop(0, PAIRS, scatter, 0)
    reduces = [
        to_x(
            1,
            step,
            acc.at[pl.ds(pl.multiple_of(lax.rem(me_p + step, PB) * 256, 256), 256)],
            share.at[pl.ds((step - 1) * 256, 256)],
        )
        for step in range(1, PB)
    ]
    for copy in reduces:
        copy.start()

    for copy in gathers:
        copy.wait_recv()
    projection = dot(hit_r[...], stk[...])
    for c in range(2):
        first, second = interleave(
            projection[:64, c * 128 : (c + 1) * 128], projection[64:, c * 128 : (c + 1) * 128]
        )
        send1[pl.ds(2 * c, 64, stride=SLOT), :] = first
        send1[pl.ds(2 * c + 1, 64, stride=SLOT), :] = second

    def to_a(stage, peer, src, dst):
        return pltpu.make_async_remote_copy(
            src_ref=src,
            dst_ref=dst,
            send_sem=a_send.at[stage],
            recv_sem=a_recv.at[stage],
            device_id={"aa": peer},
            device_id_type=pl.DeviceIdType.MESH,
        )

    def exchange(stage, source, target, count):
        def send(step, carry):
            peer = lax.rem(me_a + step, AA)
            to_a(
                stage,
                peer,
                source.at[pl.ds(pl.multiple_of(peer * SLOT, SLOT), count)],
                target.at[pl.ds(pl.multiple_of(me_a * SLOT, SLOT), count)],
            ).start()
            return carry

        lax.fori_loop(1, AA, send, 0)
        own = pl.ds(pl.multiple_of(me_a * SLOT, SLOT), count)
        target[own, :] = source[own, :]
        return to_a(
            stage,
            lax.rem(me_a + 1, AA),
            source.at[pl.ds(0, (AA - 1) * count)],
            target.at[pl.ds(0, (AA - 1) * count)],
        )

    first_move = exchange(0, send1, recv1, 5)

    others["colkey"].wait()
    for r in range(3):
        mine = lax.broadcasted_iota(jnp.int32, (64, 512), 0) + r * 64
        total = jnp.zeros((64, 512), F32)
        for e in range(LIST):
            total = total + jnp.where(colkey[e : e + 1, :] == mine, 1.0, 0.0)
        hit_c[r * 64 : (r + 1) * 64, :] = total.astype(BF16)

    others["dual"].wait()
    own_cols = pl.ds(pl.multiple_of(me_p * 256, 256), 256)
    mine = wave[own_cols, :]
    for copy in reduces:
        copy.wait_recv()
    gradient = acc[own_cols, :] + share[0:256, :] + share[256:512, :] + share[512:768, :]
    base[...] = mine - WAVE_STEP * (gradient + PENALTY * (mine + dual[...]))

    first_move.wait_recv()
    for c in range(2):
        for z in range(2):
            there = pl.ds(c * 128 + z, 64, stride=2)
            here = recv1[pl.ds(2 * c + z, 64, stride=SLOT), :]
            moved = base[there, :] + (WAVE_STEP * PENALTY) * here
            wnext[there, :] = moved
            misfit = here - (moved + dual[there, :])
            send2[pl.ds(2 * c + z, 64, stride=SLOT), :] = misfit.astype(BF16).astype(F32)
    second_move = exchange(1, send2, recv2, 4)
    wave_copy = pltpu.make_async_copy(wnext, wave_out, out_sem.at[0])
    wave_copy.start()

    own_row = pl.ds(pl.multiple_of(me_p * 8, 8), 1)
    prow[own_row, :] = jnp.sum(recv1[pl.ds(4, 64, stride=SLOT), :], axis=0, keepdims=True)
    probe_x = [to_x(3, step, prow.at[own_row], prow.at[own_row]) for step in range(1, PB)]
    for copy in probe_x:
        copy.start()
    for copy in probe_x:
        copy.wait_recv()
    pfull[pl.ds(me_a, 1), :] = (prow[0:1, :] + prow[8:9, :]) + (prow[16:17, :] + prow[24:25, :])

    def layer(step):
        peer = z_base + lax.rem(m_own + step, MESH_Y_CORE)
        row = pfull.at[pl.ds(me_a, 1)]
        return to_a(2, peer, row, row)

    for step in range(1, MESH_Y_CORE):
        layer(step).start()

    second_move.wait_recv()
    own_rays = pl.multiple_of(me_p * 128, 128)
    for c in range(2):
        first, second = interleave(
            recv2[pl.ds(2 * c, 64, stride=SLOT), :], recv2[pl.ds(2 * c + 1, 64, stride=SLOT), :]
        )
        rays[pl.ds(own_rays, 128), c * 128 : (c + 1) * 128] = jnp.concatenate(
            [first, second], axis=0
        ).astype(BF16)
    own_rows = rays.at[pl.ds(own_rays, 128)]
    ray_moves = [to_x(2, step, own_rows, own_rows) for step in range(1, PB)]
    for copy in ray_moves:
        copy.start()

    seven = pfull.at[pl.ds(0, MESH_Y_CORE - 1)]
    layer_all = to_a(2, z_base + lax.rem(m_own + 1, MESH_Y_CORE), seven, seven)
    layer_all.wait_recv()
    layer_all.wait_send()
    group = pfull.at[pl.ds(pl.multiple_of(z_base, 8), 8)]

    def stack(step):
        peer = lax.rem(z_own + step, AA // MESH_Y_CORE) * MESH_Y_CORE + m_own
        return to_a(3, peer, group, group)

    for step in range(1, AA // MESH_Y_CORE):
        stack(step).start()

    for copy in ray_moves:
        copy.wait_recv()

    sums = dot(hit_c[...], rays[...]).astype(BF16).astype(F32)
    for t in range(6):
        for br in range(2):
            for c in range(2):
                at = 2 * t * 16 + br * 8
                first, second = interleave(
                    sums[at : at + 8, c * 128 : (c + 1) * 128],
                    sums[at + 16 : at + 24, c * 128 : (c + 1) * 128],
                )
                spread[pl.ds(t * 64 + 4 * c + br, 8, stride=8), :] = first
                spread[pl.ds(t * 64 + 4 * c + 2 + br, 8, stride=8), :] = second
    table = jnp.concatenate(
        [spread[t * 64 : (t + 1) * 64, :] for t in range(6)], axis=1
    ).astype(BF16)
    for n in range(WCH):
        grad = lax.dot_general(
            table,
            wts[n * WROWS : (n + 1) * WROWS, :],
            (((1,), (1,)), ((), ())),
            preferred_element_type=F32,
        )
        for s in range(per):
            q = n * per + s
            for t in range(4):
                first, second = interleave(
                    grad[t * 16 : t * 16 + 8, s * 128 : (s + 1) * 128],
                    grad[t * 16 + 8 : t * 16 + 16, s * 128 : (s + 1) * 128],
                )
                even = pl.ds(t * 512 + 2 * q, 8, stride=64)
                odd = pl.ds(t * 512 + 2 * q + 1, 8, stride=64)
                onew[even, :] = obj[even, :] - OBJECT_STEP * first
                onew[odd, :] = obj[odd, :] - OBJECT_STEP * second
    obj_copies = [
        pltpu.make_async_copy(
            onew.at[pl.ds(t * 512, 512)], obj_out.at[:, pl.ds(t * 128, 128)], out_sem.at[1 + t]
        )
        for t in range(4)
    ]
    for copy in obj_copies:
        copy.start()

    others_all = pfull.at[pl.ds(0, 7 * MESH_Y_CORE)]
    stack_all = to_a(
        3, lax.rem(z_own + 1, AA // MESH_Y_CORE) * MESH_Y_CORE + m_own, others_all, others_all
    )
    stack_all.wait_recv()
    stack_all.wait_send()
    total = pfull[...]
    scale = PROBE_STEP / (AA * POS * PB)
    old_re, old_im = probe[0], probe[1]
    pout[0] = (old_re - scale * total)[:, :64]
    pout[1] = (old_im - scale * swap(total))[:, :64]
    probe_copy = pltpu.make_async_copy(pout, probe_out, out_sem.at[5])
    probe_copy.start()

    for copy in gathers + reduces + probe_x + ray_moves:
        copy.wait_send()
    first_move.wait_send()
    second_move.wait_send()
    wave_copy.wait()
    for copy in obj_copies:
        copy.wait()
    probe_copy.wait()


def shards(
    tables,
    wave_field,
    scaled_dual,
    intensity,
    probe_field,
    scan_rows,
    scan_cols,
    sample_mask,
    object_field,
    ray_blocks,
    ray_tables,
    radon_weights,
):
    column = lax.axis_index("pb")
    own_blocks = 64 // PB
    place = ray_tables * own_blocks + ray_blocks % own_blocks
    owner = ray_blocks // own_blocks
    own_lists = lax.dynamic_slice_in_dim(owner * KEYS + place, column * 2, 2, 1)
    row_keys = own_lists.transpose(1, 0, 2).reshape(2 * AA, LIST)
    col_keys = jnp.where(owner == column, place, -1).transpose(2, 1, 0).reshape(LIST, NB * AA)
    any_spec = pl.BlockSpec(memory_space=pl.ANY)
    smem = pl.BlockSpec(memory_space=pltpu.SMEM)
    vmem = pltpu.VMEM
    wave_next, probe_next, object_next = pl.pallas_call(
        kernel,
        out_shape=(
            jax.ShapeDtypeStruct((256, 128), F32),
            jax.ShapeDtypeStruct((2, 64, 64), F32),
            jax.ShapeDtypeStruct((512, 512), F32),
        ),
        in_specs=[smem] * 3 + [any_spec] * 9,
        out_specs=[any_spec] * 3,
        scratch_shapes=[
            vmem((2048, 128), F32),
            vmem((4096, 768), BF16),
            vmem((1024, 128), F32),
            vmem((256, 128), F32),
            vmem((POS, 32, 128), F32),
            vmem((2, 64, 128), F32),
            vmem((6, 256, 256), BF16),
            vmem((128, LIST), jnp.int32),
            vmem((LIST, 512), jnp.int32),
            vmem((2048, 128), F32),
            vmem((384, 128), F32),
            vmem((768, 256), BF16),
            vmem((128, 768), BF16),
            vmem((KEYS, 512), BF16),
            vmem((512, 128), F32),
            vmem((512, 128), F32),
            vmem((512, 128), F32),
            vmem((512, 128), F32),
            vmem((768, 128), F32),
            vmem((1024, 128), F32),
            vmem((768, 128), F32),
            vmem((256, 128), F32),
            vmem((AA * SLOT, 128), F32),
            vmem((AA * SLOT, 128), F32),
            vmem((AA * SLOT, 128), F32),
            vmem((AA * SLOT, 128), F32),
            vmem((256, 128), F32),
            vmem((512, 256), BF16),
            vmem((384, 128), F32),
            vmem((2048, 128), F32),
            vmem((32, 128), F32),
            vmem((64, 128), F32),
            vmem((2, 64, 64), F32),
            pltpu.SemaphoreType.DMA((14,)),
            pltpu.SemaphoreType.DMA((WCH,)),
            pltpu.SemaphoreType.DMA((6,)),
            pltpu.SemaphoreType.DMA((12,)),
            pltpu.SemaphoreType.DMA((12,)),
            pltpu.SemaphoreType.DMA((4,)),
            pltpu.SemaphoreType.DMA((4,)),
        ],
        compiler_params=pltpu.CompilerParams(
            collective_id=0, has_side_effects=True, vmem_limit_bytes=48 * 1024 * 1024
        ),
        name="admm",
    )(
        scan_rows,
        scan_cols,
        sample_mask,
        object_field.reshape(512, 512),
        radon_weights,
        wave_field.reshape(256, 512),
        scaled_dual.reshape(256, 128),
        intensity.reshape(POS, 32, 128),
        jnp.concatenate([probe_field, probe_field], axis=2),
        tables,
        row_keys,
        col_keys,
    )
    return (
        wave_next.reshape(1, 2, 128, 128),
        probe_next,
        object_next.reshape(2, 2, 128, 512),
    )


def solution(mesh):
    specs = (
        P("aa", None, None, None),
        P("aa", None, None, "pb"),
        P("aa", "pb", None),
        P(),
        P("aa", "pb"),
        P("aa", "pb"),
        P("aa", "pb"),
        P(None, "aa", "pb", None),
        P(),
        P(),
        P(),
    )
    mapped = jax.shard_map(
        shards,
        mesh=mesh,
        in_specs=(P(),) + specs,
        out_specs=(P("aa", None, None, "pb"), P(), P(None, "aa", "pb", None)),
        check_vma=False,
    )

    def step(*arrays):
        return mapped(jnp.asarray(dft_constants()), *arrays)

    return step
```

time: 385 us -> 58.2 us (0.15)
  local copies, waits for them, and re-layouts: 128 us -> 9.7 us
  blocking collectives: 92.2 us -> 0 us
  other arithmetic: 84.1 us -> 1.89 us
  Pallas kernels: 0 us -> 45.5 us
  matrix products: 32.1 us -> 0 us
  waiting for transfers between devices: 19.9 us -> 0 us
  between operations: 14.6 us -> 0.67 us
  starting transfers between devices: 10.2 us -> 0 us
    psum x1 -> x0, blocking collectives: 83.1 us -> none  [shards(): probe_total = lax.psum(probe_grad, ('aa', 'pb'))]
    scatter-add x32 -> x0, other arithmetic: 71.9 us -> none
    scatter-add x48 -> x0, local copies, waits for them, and re-layouts: 54.7 us -> none
    pallas_call x0 -> x1, Pallas kernels: none -> 45.5 us  [shards(): pl.pallas_call(kernel, out_shape=(jax.ShapeDtypeStruct((256, 128), F32),...]
    gather x48 -> x0, local copies, waits for them, and re-layouts: 44.9 us -> none
    dot_general x20 -> x0, matrix products: 32.1 us -> none  [the longest x8 8.54 us: apply_left(): return jnp.einsum('ik,nkl->nil', table, field, precision=highest)]
    reshape x14 -> x1, local copies, waits for them, and re-layouts: 22.5 us -> 0.08 us  [shards(): jnp.where(owner == column, place, -1).transpose(2, 1, 0)]
    all_to_all x2 -> x0, waiting for transfers between devices: 19.8 us -> none  [the longest x1 10.2 us: shards(): lax.all_to_all(target, 'aa', split_axis=2, concat_axis=0, tiled=True)]
  transfers between devices with their start and end apart: 4 -> 0, of which waited for: 2 -> 0; matrix products, arithmetic and copies ran while one was open for 59% -> 0% of each run, Pallas kernels for 0% -> 0%
where the time goes in v1:
time: 58.2 us; the launch traced here: 57.8 us
  Pallas kernels  45.5 us (78%)
  local copies, waits for them, and re-layouts  9.7 us (17%)
  other arithmetic  1.89 us (3%)
  between operations  0.67 us (1%)
    pallas_call x1, Pallas kernels, shards(): pl.pallas_call(kernel, out_shape=(jax.ShapeDtypeStruct((256, 128), F32),...  45.5 us
    unnamed x18, local copies, waits for them, and re-layouts  9.52 us

profile of v1, /device:TPU:1, one launch (start us, length us, event | category | flops | bytes accessed | tf_op | source)
XLA Modules:
  0.0 57.8 jit_solution(11901351979150503315)
XLA Ops:
  0.6 1.0 %pad_maximum_fusion.probe_hbm = f32[2,64,128]{2,1,0:T(8,128)S(1)} fusion(f32[2,64,64]{2,1,0:T(8,128)} %param.15), kind=kLoop, calls=%fused_computation.5 | loop fusion | flops 16384 | bytes 98304 | tf_op jit(solution)/shard_map/concatenate | solution.py:652
  1.6 0.9 %select_bitcast_fusion = (s32[12,8,64]{2,1,0:T(8,128)S(1)}, s32[64,8,12]{0,1,2:T(8,128)S(1)}, s32[64,8,12]{0,1,2:T(8,128)S(1)}) fusion(s32[]{:T(128)S(6)} %axis_index.12, s32[64,8,12]{0,1,2:T(8,128)} %param.20, s32[64,8,12]{0,1,2:T(8,128)} %param.21), kind=kLoop, calls=%fused_computation.7 | loop fusion | flops 141312 | bytes 122884 | tf_op jit(solution)/shard_map/transpose | solution.py:584
  2.5 0.1 reshape.35.colkey_hbm
  2.6 0.1 copy.15
  2.7 1.0 %copy.16 = f32[2,8,32,128]{3,2,1,0:T(8,128)S(1)} copy(f32[2,8,32,128]{3,1,2,0:T(8,128)} %bitcast.20) | data formatting | bytes 524288
  3.7 0.0 copy-start
  3.7 1.2 %copy-done = f32[2,2,128,512]{3,2,1,0:T(8,128)S(1)} copy-done((f32[2,2,128,512]{3,2,1,0:T(8,128)S(1)}, f32[2,2,128,512]{3,2,1,0:T(8,128)}, u32[]{:S(2)}) %copy-start) | copy-done | bytes 1048600
  4.9 0.0 copy-start.1
  5.0 1.1 %copy-done.1 = bf16[6,256,256]{2,1,0:T(8,128)(2,1)S(1)} copy-done((bf16[6,256,256]{2,1,0:T(8,128)(2,1)S(1)}, bf16[6,256,256]{2,1,0:T(8,128)(2,1)}, u32[]{:S(2)}) %copy-start.1) | copy-done | bytes 786456
  6.1 0.0 copy-start.2
  6.1 1.0 %copy-done.2 = f32[1,2,128,512]{3,2,1,0:T(8,128)S(1)} copy-done((f32[1,2,128,512]{3,2,1,0:T(8,128)S(1)}, f32[1,2,128,512]{3,2,1,0:T(8,128)}, u32[]{:S(2)}) %copy-start.2) | copy-done | bytes 524312
  7.1 0.0 copy-start.3
  7.1 0.9 %copy-done.3 = f32[1,2,128,128]{3,2,1,0:T(8,128)S(1)} copy-done((f32[1,2,128,128]{3,2,1,0:T(8,128)S(1)}, f32[1,2,128,128]{3,2,1,0:T(8,128)}, u32[]{:S(2)}) %copy-start.3) | copy-done | bytes 131096
  8.0 0.0 copy-start.4
  8.0 0.7 %copy-done.4 = s32[1,16]{1,0:T(1,128)S(1)} copy-done((s32[1,16]{1,0:T(1,128)S(1)}, s32[1,16]{1,0:T(1,128)}, u32[]{:S(2)}) %copy-start.4) | copy-done | bytes 88
  8.7 0.0 copy-start.5
  8.7 0.7 %copy-done.5 = s32[1,16]{1,0:T(1,128)S(1)} copy-done((s32[1,16]{1,0:T(1,128)S(1)}, s32[1,16]{1,0:T(1,128)}, u32[]{:S(2)}) %copy-start.5) | copy-done | bytes 88
  9.3 0.0 copy-start.6
  9.3 0.7 %copy-done.6 = s32[1,16]{1,0:T(1,128)S(1)} copy-done((s32[1,16]{1,0:T(1,128)S(1)}, s32[1,16]{1,0:T(1,128)}, u32[]{:S(2)}) %copy-start.6) | copy-done | bytes 88
  10.0 45.5 %admm.1 = (f32[256,128]{1,0:T(8,128)S(1)}, f32[2,64,64]{2,1,0:T(8,128)S(1)}, f32[512,512]{1,0:T(8,128)S(1)}) custom-call(s32[1,16]{1,0:T(1,128)S(1)} %copy-done.4, s32[1,16]{1,0:T(1,128)S(1)} %copy-done.5, s32[1,16]{1,0:T(1,128)S(1)} %copy-done.6, f32[512,512]{1,0:T(8,128)S(1)} %bitcast.13, bf16[4096,768]{1,0:T(8,128)(2,1)} %wts_hbm.1, ...), custom_call_target="tpu_custom_call" | custom-call | tf_op jit(solution)/shard_map/admm/pallas_call | solution.py:588
  55.6 0.7 %copy.20 = f32[1,2,128,128]{3,2,1,0:T(8,128)} copy(f32[1,2,128,128]{3,2,1,0:T(8,128)S(1)} %bitcast.19) | data formatting | bytes 262144
  56.2 0.6 %copy.21 = f32[2,64,64]{2,1,0:T(8,128)} copy(f32[2,64,64]{2,1,0:T(8,128)S(1)} %get-tuple-element.16) | data formatting | bytes 65536
  56.8 1.0 %copy.22 = f32[2,2,128,512]{3,2,1,0:T(8,128)} copy(f32[2,2,128,512]{3,2,1,0:T(8,128)S(1)} %bitcast.15) | data formatting | bytes 2097152
  (1 shorter events, 0.0 us)
Async XLA Ops:
  3.7 1.2 %copy-start = (f32[2,2,128,512]{3,2,1,0:T(8,128)S(1)}, f32[2,2,128,512]{3,2,1,0:T(8,128)}, u32[]{:S(2)}) copy-start(f32[2,2,128,512]{3,2,1,0:T(8,128)} %param.19) | copy-start | bytes 3145732
  4.9 1.1 %copy-start.1 = (bf16[6,256,256]{2,1,0:T(8,128)(2,1)S(1)}, bf16[6,256,256]{2,1,0:T(8,128)(2,1)}, u32[]{:S(2)}) copy-start(bf16[6,256,256]{2,1,0:T(8,128)(2,1)} %constant.43.clone.tab_hbm) | copy-start | bytes 2359300
  6.1 1.0 %copy-start.2 = (f32[1,2,128,512]{3,2,1,0:T(8,128)S(1)}, f32[1,2,128,512]{3,2,1,0:T(8,128)}, u32[]{:S(2)}) copy-start(f32[1,2,128,512]{3,2,1,0:T(8,128)} %param.12) | copy-start | bytes 1572868
  7.1 0.9 %copy-start.3 = (f32[1,2,128,128]{3,2,1,0:T(8,128)S(1)}, f32[1,2,128,128]{3,2,1,0:T(8,128)}, u32[]{:S(2)}) copy-start(f32[1,2,128,128]{3,2,1,0:T(8,128)} %param.13) | copy-start | bytes 393220
  8.0 0.7 %copy-start.4 = (s32[1,16]{1,0:T(1,128)S(1)}, s32[1,16]{1,0:T(1,128)}, u32[]{:S(2)}) copy-start(s32[1,16]{1,0:T(1,128)} %rows_ref.1) | copy-start | bytes 196
  8.7 0.7 %copy-start.5 = (s32[1,16]{1,0:T(1,128)S(1)}, s32[1,16]{1,0:T(1,128)}, u32[]{:S(2)}) copy-start(s32[1,16]{1,0:T(1,128)} %cols_ref.1) | copy-start | bytes 196
  9.3 0.7 %copy-start.6 = (s32[1,16]{1,0:T(1,128)S(1)}, s32[1,16]{1,0:T(1,128)}, u32[]{:S(2)}) copy-start(s32[1,16]{1,0:T(1,128)} %mask_ref.1) | copy-start | bytes 196

commit v2 on v1

--- a/solution.py
+++ b/solution.py
@@ -2,7 +2,6 @@
 
 import jax
 import jax.numpy as jnp
-import ml_dtypes
 import numpy as np
 from jax import lax
 from jax.experimental import pallas as pl
@@ -18,11 +17,15 @@
 ZC = 4
 POS = 16
 PAIRS = 8
+OWN = 64 // PB
 KEYS = 192
-MESH_Y_CORE = 8
-SLOT = 8
+LAYER = 8
+DEPTH = 8
+SLOT = 40
+SLOT2 = 32
 WCH = 8
 WROWS = 4096 // WCH
+OUTS = 4
 
 WAVE_STEP = 0.05
 PENALTY = 1.0
@@ -31,12 +34,6 @@
 
 F32 = jnp.float32
 BF16 = jnp.bfloat16
-
-
-def split_np(table):
-    high = table.astype(ml_dtypes.bfloat16)
-    low = (table - high.astype(np.float64)).astype(ml_dtypes.bfloat16)
-    return high, low
 
 
 def dft_constants():
@@ -51,17 +48,14 @@
         return np.block([[dre, dim], [-dim, dre]])
 
     def left(re, im):
-        high, low = split_np(np.block([[re, -im], [im, re]]))
-        return np.concatenate(
-            [np.concatenate([high, high], 1), np.concatenate([low, low], 1)], 0
-        )
+        return np.block([[re, -im], [im, re]])
 
     order = np.concatenate([np.arange(0, BLK, 2), np.arange(1, BLK, 2)])
-    g_hi, g_lo = split_np(right(f_re, f_im))
-    b_hi, b_lo = split_np(right(f_re, -f_im))
-    l_fwd = left(f_re[order, :], f_im[order, :])
-    l_bwd = left(f_re[:, order], -f_im[:, order])
-    return np.stack([g_hi, g_lo, b_hi, b_lo, l_fwd, l_bwd])
+    rights = [right(f_re, f_im), right(f_re, -f_im)]
+    lefts = np.concatenate(
+        [left(f_re[order, :], f_im[order, :]), left(f_re[:, order], -f_im[:, order])], axis=1
+    )
+    return np.concatenate(rights + [lefts], axis=0).astype(np.float32)
 
 
 def halves(value):
@@ -115,19 +109,22 @@
     int_hbm,
     probe_hbm,
     tab_hbm,
-    rowkey_hbm,
-    colkey_hbm,
-    wave_out,
-    probe_out,
-    obj_out,
+    blocks_hbm,
+    tables_hbm,
+    wts,
     obj,
-    wts,
+    wnext,
+    pfull,
+    table,
     wave,
     dual,
+    int_raw,
     inten,
     probe,
+    tab_raw,
     tab,
-    rowkey,
+    blocks,
+    tables,
     colkey,
     lhs,
     ptile,
@@ -143,19 +140,20 @@
     share,
     base,
     send1,
+    mid1,
+    turn1,
     recv1,
+    loose,
     send2,
+    mid2,
+    loose2,
+    turn2,
     recv2,
-    wnext,
     rays,
     spread,
-    onew,
     prow,
-    pfull,
-    pout,
     in_sem,
     w_sem,
-    out_sem,
     x_send,
     x_recv,
     a_send,
@@ -163,9 +161,15 @@
 ):
     me_a = lax.axis_index("aa")
     me_p = lax.axis_index("pb")
-    z_base = (me_a // MESH_Y_CORE) * MESH_Y_CORE
-    z_own = me_a // MESH_Y_CORE
-    m_own = me_a % MESH_Y_CORE
+    z_own = me_a // LAYER
+    m_own = me_a % LAYER
+    z_base = z_own * LAYER
+
+    def layer_peer(step):
+        return z_base + lax.rem(m_own + step, LAYER)
+
+    def depth_peer(step):
+        return lax.rem(z_own + step, DEPTH) * LAYER + m_own
 
     def lanes(shape):
         return lax.broadcasted_iota(jnp.int32, shape, 1)
@@ -192,31 +196,29 @@
         name: pltpu.make_async_copy(src, dst, in_sem.at[8 + n])
         for n, (name, src, dst) in enumerate(
             [
-                ("rowkey", rowkey_hbm, rowkey),
-                ("colkey", colkey_hbm, colkey),
+                ("blocks", blocks_hbm, blocks),
+                ("tables", tables_hbm, tables),
                 ("probe", probe_hbm, probe),
-                ("tab", tab_hbm, tab),
-                ("inten", int_hbm, inten),
+                ("tab", tab_hbm, tab_raw),
+                ("inten", int_hbm, int_raw),
                 ("dual", dual_hbm, dual),
             ]
         )
     }
-    others["rowkey"].start()
+    others["blocks"].start()
+    others["tables"].start()
     for copy in obj_in + wts_in + wave_in:
         copy.start()
-    for name in ("probe", "tab", "inten", "dual", "colkey"):
+    for name in ("probe", "tab", "inten", "dual"):
         others[name].start()
 
     barrier = pltpu.get_barrier_semaphore()
 
-    def greet(step, carry):
-        peer = lax.rem(me_a + step, AA)
-        pl.semaphore_signal(
-            barrier, inc=1, device_id={"aa": peer}, device_id_type=pl.DeviceIdType.MESH
-        )
-        return carry
-
-    lax.fori_loop(1, AA, greet, 0)
+    for step in range(1, LAYER):
+        for peer in (layer_peer(step), depth_peer(step)):
+            pl.semaphore_signal(
+                barrier, inc=1, device_id={"aa": peer}, device_id_type=pl.DeviceIdType.MESH
+            )
     for step in range(1, PB):
         pl.semaphore_signal(
             barrier,
@@ -225,8 +227,17 @@
             device_id_type=pl.DeviceIdType.MESH,
         )
 
-    others["rowkey"].wait()
-    keys = rowkey[...]
+    others["blocks"].wait()
+    others["tables"].wait()
+    keys = []
+    for jj in range(2):
+        there = pl.ds(me_p * 2 + jj, LIST, stride=NB)
+        block = blocks[there, :]
+        keys.append((block // OWN) * KEYS + tables[there, :] * OWN + block % OWN)
+    keys = jnp.concatenate(
+        [jnp.concatenate(keys, axis=1), jnp.zeros((128 - LIST, 128), jnp.int32)], axis=0
+    )
+    keys = jnp.transpose(keys.astype(F32)).astype(jnp.int32)
     for t in range(6):
         column = lanes((128, 128)) + t * 128
         total = jnp.zeros((128, 128), F32)
@@ -273,7 +284,7 @@
                     c * 128 : (c + 1) * 128,
                 ] = jnp.concatenate(lists[h][c], axis=0).astype(BF16)
 
-    pl.semaphore_wait(barrier, AA - 1 + PB - 1)
+    pl.semaphore_wait(barrier, LAYER - 1 + DEPTH - 1 + PB - 1)
 
     def to_x(stage, step, src, dst):
         peer = lax.rem(me_p + step, PB)
@@ -290,6 +301,21 @@
     gathers = [to_x(0, step, own_block, own_block) for step in range(1, PB)]
     for copy in gathers:
         copy.start()
+
+    def scatter_rows(ref, slot, k, value):
+        for h in range(8):
+            ref[pl.ds(k * 8 + h, 8, stride=slot), :] = value[h * 8 : (h + 1) * 8]
+
+    def turn_rows(source, target, slot):
+        for h in range(8):
+            target[h * slot : h * slot + 32, :] = jnp.concatenate(
+                [source[pl.ds(k * 8 + h, 8, stride=slot), :] for k in range(4)], axis=0
+            ).astype(target.dtype)
+
+    def gather_rows(value, slot, k):
+        return jnp.concatenate(
+            [value[h * slot + k * 8 : h * slot + k * 8 + 8] for h in range(8)], axis=0
+        )
 
     for copy in wave_in:
         copy.wait()
@@ -314,8 +340,21 @@
     others["probe"].wait()
     others["tab"].wait()
     others["inten"].wait()
-    p_re = jnp.concatenate([probe[0]] * PAIRS, axis=0)
-    p_im = jnp.concatenate([probe[1]] * PAIRS, axis=0)
+    for octet in range(2):
+        for t in range(32):
+            inten[pl.ds(octet * 256 + t, 8, stride=32), :] = int_raw[
+                octet * 8 : octet * 8 + 8, t * 128 : (t + 1) * 128
+            ]
+    for n in range(2):
+        tab[2 * n], tab[2 * n + 1] = halves(tab_raw[n * 256 : (n + 1) * 256, :])
+        high, low = halves(tab_raw[512:640, n * 128 : (n + 1) * 128])
+        tab[4 + n] = jnp.concatenate(
+            [jnp.concatenate([high] * 2, axis=1), jnp.concatenate([low] * 2, axis=1)], axis=0
+        )
+    one_re = jnp.concatenate([probe[0]] * 2, axis=1)
+    one_im = jnp.concatenate([probe[1]] * 2, axis=1)
+    p_re = jnp.concatenate([one_re] * PAIRS, axis=0)
+    p_im = jnp.concatenate([one_im] * PAIRS, axis=0)
     w_re, w_im = win_r[...], win_i[...]
     half_re, half_im = right_apply(
         p_re * w_re - p_im * w_im, p_re * w_im + p_im * w_re, tab[0], tab[1]
@@ -323,7 +362,9 @@
     far_re, far_im = left_apply(rows_to_lanes(half_re), rows_to_lanes(half_im), tab[4])
     measured, live = [], []
     for q in range(PAIRS):
-        even, odd = interleave(inten[2 * q], inten[2 * q + 1])
+        even, odd = interleave(
+            inten[2 * q * 32 : 2 * q * 32 + 32, :], inten[2 * q * 32 + 32 : 2 * q * 32 + 64, :]
+        )
         measured.append(jnp.concatenate([even, odd], axis=0))
         live.append(
             jnp.where(
@@ -341,7 +382,7 @@
     grad_im = jnp.sum((w_re * back_im - w_im * back_re).reshape(PAIRS, 64, 128), axis=0)
     grad_re = grad_re + swap(grad_re)
     grad_im = grad_im + swap(grad_im)
-    send1[pl.ds(4, 64, stride=SLOT), :] = jnp.where(lanes((64, 128)) < 64, grad_re, grad_im)
+    scatter_rows(send1, SLOT, 4, jnp.where(lanes((64, 128)) < 64, grad_re, grad_im))
 
     pad[...] = jnp.zeros_like(pad)
     acc[...] = jnp.zeros_like(acc)
@@ -384,8 +425,8 @@
         first, second = interleave(
             projection[:64, c * 128 : (c + 1) * 128], projection[64:, c * 128 : (c + 1) * 128]
         )
-        send1[pl.ds(2 * c, 64, stride=SLOT), :] = first
-        send1[pl.ds(2 * c + 1, 64, stride=SLOT), :] = second
+        scatter_rows(send1, SLOT, 2 * c, first)
+        scatter_rows(send1, SLOT, 2 * c + 1, second)
 
     def to_a(stage, peer, src, dst):
         return pltpu.make_async_remote_copy(
@@ -397,36 +438,49 @@
             device_id_type=pl.DeviceIdType.MESH,
         )
 
-    def exchange(stage, source, target, count):
-        def send(step, carry):
-            peer = lax.rem(me_a + step, AA)
+    def exchange(stage, source, target, slot, count):
+        own = (m_own, z_own)[stage % 2]
+        for step in range(1, 8):
+            there = lax.rem(own + step, 8)
             to_a(
                 stage,
-                peer,
-                source.at[pl.ds(pl.multiple_of(peer * SLOT, SLOT), count)],
-                target.at[pl.ds(pl.multiple_of(me_a * SLOT, SLOT), count)],
+                (layer_peer, depth_peer)[stage % 2](step),
+                source.at[pl.ds(pl.multiple_of(there * slot, 8), count)],
+                target.at[pl.ds(pl.multiple_of(own * slot, 8), count)],
             ).start()
-            return carry
-
-        lax.fori_loop(1, AA, send, 0)
-        own = pl.ds(pl.multiple_of(me_a * SLOT, SLOT), count)
-        target[own, :] = source[own, :]
+        here = pl.ds(pl.multiple_of(own * slot, 16 if slot == SLOT2 else 8), count)
+        target[here, :] = source[here, :]
         return to_a(
             stage,
-            lax.rem(me_a + 1, AA),
-            source.at[pl.ds(0, (AA - 1) * count)],
-            target.at[pl.ds(0, (AA - 1) * count)],
-        )
-
-    first_move = exchange(0, send1, recv1, 5)
-
-    others["colkey"].wait()
+            (layer_peer, depth_peer)[stage % 2](1),
+            source.at[pl.ds(0, 7 * count)],
+            target.at[pl.ds(0, 7 * count)],
+        )
+
+    moves = [exchange(0, send1, mid1, SLOT, SLOT)]
+
+    for p in range(PB):
+        parts = []
+        for jj in range(2):
+            there = pl.ds(p * 2 + jj, LIST, stride=NB)
+            block = blocks[there, :]
+            place = tables[there, :] * OWN + block % OWN
+            parts.append(jnp.where(block // OWN == me_p, place, -1))
+        colkey[:, p * 128 : (p + 1) * 128] = jnp.concatenate(parts, axis=1)
     for r in range(3):
         mine = lax.broadcasted_iota(jnp.int32, (64, 512), 0) + r * 64
         total = jnp.zeros((64, 512), F32)
         for e in range(LIST):
             total = total + jnp.where(colkey[e : e + 1, :] == mine, 1.0, 0.0)
         hit_c[r * 64 : (r + 1) * 64, :] = total.astype(BF16)
+
+    moves[0].wait_recv()
+    turn_rows(mid1, turn1, SLOT)
+    partial = mid1[32:40, :]
+    for l in range(1, 8):
+        partial = partial + mid1[l * SLOT + 32 : l * SLOT + 40, :]
+    turn1[pl.ds(32, 8, stride=SLOT), :] = partial
+    moves.append(exchange(1, turn1, recv1, SLOT, 33))
 
     others["dual"].wait()
     own_cols = pl.ds(pl.multiple_of(me_p * 256, 256), 256)
@@ -436,41 +490,44 @@
     gradient = acc[own_cols, :] + share[0:256, :] + share[256:512, :] + share[512:768, :]
     base[...] = mine - WAVE_STEP * (gradient + PENALTY * (mine + dual[...]))
 
-    first_move.wait_recv()
+    moves[1].wait_recv()
     for c in range(2):
         for z in range(2):
             there = pl.ds(c * 128 + z, 64, stride=2)
-            here = recv1[pl.ds(2 * c + z, 64, stride=SLOT), :]
+            here = gather_rows(recv1, SLOT, 2 * c + z)
             moved = base[there, :] + (WAVE_STEP * PENALTY) * here
             wnext[there, :] = moved
-            misfit = here - (moved + dual[there, :])
-            send2[pl.ds(2 * c + z, 64, stride=SLOT), :] = misfit.astype(BF16).astype(F32)
-    second_move = exchange(1, send2, recv2, 4)
-    wave_copy = pltpu.make_async_copy(wnext, wave_out, out_sem.at[0])
-    wave_copy.start()
+            scatter_rows(loose, SLOT2, 2 * c + z, here - (moved + dual[there, :]))
+    send2[...] = loose[...].astype(BF16)
+    moves.append(exchange(2, send2, mid2, SLOT2, SLOT2))
 
     own_row = pl.ds(pl.multiple_of(me_p * 8, 8), 1)
-    prow[own_row, :] = jnp.sum(recv1[pl.ds(4, 64, stride=SLOT), :], axis=0, keepdims=True)
+    prow[own_row, :] = jnp.sum(recv1[pl.ds(32, 8, stride=SLOT), :], axis=0, keepdims=True)
     probe_x = [to_x(3, step, prow.at[own_row], prow.at[own_row]) for step in range(1, PB)]
     for copy in probe_x:
         copy.start()
+    moves[2].wait_recv()
+    loose2[...] = mid2[...].astype(F32)
+    turn_rows(loose2, turn2, SLOT2)
+    moves.append(exchange(3, turn2, recv2, SLOT2, SLOT2))
+
     for copy in probe_x:
         copy.wait_recv()
     pfull[pl.ds(me_a, 1), :] = (prow[0:1, :] + prow[8:9, :]) + (prow[16:17, :] + prow[24:25, :])
 
     def layer(step):
-        peer = z_base + lax.rem(m_own + step, MESH_Y_CORE)
         row = pfull.at[pl.ds(me_a, 1)]
-        return to_a(2, peer, row, row)
-
-    for step in range(1, MESH_Y_CORE):
+        return to_a(4, layer_peer(step), row, row)
+
+    for step in range(1, LAYER):
         layer(step).start()
 
-    second_move.wait_recv()
+    moves[3].wait_recv()
     own_rays = pl.multiple_of(me_p * 128, 128)
+    arrived = recv2[...].astype(F32)
     for c in range(2):
         first, second = interleave(
-            recv2[pl.ds(2 * c, 64, stride=SLOT), :], recv2[pl.ds(2 * c + 1, 64, stride=SLOT), :]
+            gather_rows(arrived, SLOT2, 2 * c), gather_rows(arrived, SLOT2, 2 * c + 1)
         )
         rays[pl.ds(own_rays, 128), c * 128 : (c + 1) * 128] = jnp.concatenate(
             [first, second], axis=0
@@ -480,17 +537,16 @@
     for copy in ray_moves:
         copy.start()
 
-    seven = pfull.at[pl.ds(0, MESH_Y_CORE - 1)]
-    layer_all = to_a(2, z_base + lax.rem(m_own + 1, MESH_Y_CORE), seven, seven)
+    seven = pfull.at[pl.ds(0, LAYER - 1)]
+    layer_all = to_a(4, layer_peer(1), seven, seven)
     layer_all.wait_recv()
     layer_all.wait_send()
     group = pfull.at[pl.ds(pl.multiple_of(z_base, 8), 8)]
 
     def stack(step):
-        peer = lax.rem(z_own + step, AA // MESH_Y_CORE) * MESH_Y_CORE + m_own
-        return to_a(3, peer, group, group)
-
-    for step in range(1, AA // MESH_Y_CORE):
+        return to_a(5, depth_peer(step), group, group)
+
+    for step in range(1, DEPTH):
         stack(step).start()
 
     for copy in ray_moves:
@@ -507,12 +563,53 @@
                 )
                 spread[pl.ds(t * 64 + 4 * c + br, 8, stride=8), :] = first
                 spread[pl.ds(t * 64 + 4 * c + 2 + br, 8, stride=8), :] = second
-    table = jnp.concatenate(
+    table[...] = jnp.concatenate(
         [spread[t * 64 : (t + 1) * 64, :] for t in range(6)], axis=1
     ).astype(BF16)
+
+    others_all = pfull.at[pl.ds(0, 7 * LAYER)]
+    stack_all = to_a(5, depth_peer(1), others_all, others_all)
+    stack_all.wait_recv()
+    stack_all.wait_send()
+    for copy in gathers + reduces + probe_x + ray_moves:
+        copy.wait_send()
+    for copy in moves:
+        copy.wait_send()
+
+
+def tail(
+    probe_hbm,
+    wts,
+    obj,
+    wnext,
+    pfull,
+    table,
+    wave_out,
+    probe_out,
+    obj_out,
+    onew,
+    probe,
+    pout,
+    sem,
+):
+    probe_in = pltpu.make_async_copy(probe_hbm, probe, sem.at[0])
+    probe_in.start()
+    wave_copy = pltpu.make_async_copy(wnext, wave_out, sem.at[1])
+    wave_copy.start()
+
+    probe_in.wait()
+    scale = PROBE_STEP / (AA * POS * PB)
+    pout[0] = probe[0] - scale * pfull[:, :64]
+    pout[1] = probe[1] - scale * swap(pfull[...])[:, :64]
+    probe_copy = pltpu.make_async_copy(pout, probe_out, sem.at[2])
+    probe_copy.start()
+
+    per = 32 // WCH
+    rows = 64 // OUTS
+    obj_copies = []
     for n in range(WCH):
         grad = lax.dot_general(
-            table,
+            table[...],
             wts[n * WROWS : (n + 1) * WROWS, :],
             (((1,), (1,)), ((), ())),
             preferred_element_type=F32,
@@ -528,37 +625,20 @@
                 odd = pl.ds(t * 512 + 2 * q + 1, 8, stride=64)
                 onew[even, :] = obj[even, :] - OBJECT_STEP * first
                 onew[odd, :] = obj[odd, :] - OBJECT_STEP * second
-    obj_copies = [
-        pltpu.make_async_copy(
-            onew.at[pl.ds(t * 512, 512)], obj_out.at[:, pl.ds(t * 128, 128)], out_sem.at[1 + t]
-        )
-        for t in range(4)
-    ]
-    for copy in obj_copies:
-        copy.start()
-
-    others_all = pfull.at[pl.ds(0, 7 * MESH_Y_CORE)]
-    stack_all = to_a(
-        3, lax.rem(z_own + 1, AA // MESH_Y_CORE) * MESH_Y_CORE + m_own, others_all, others_all
-    )
-    stack_all.wait_recv()
-    stack_all.wait_send()
-    total = pfull[...]
-    scale = PROBE_STEP / (AA * POS * PB)
-    old_re, old_im = probe[0], probe[1]
-    pout[0] = (old_re - scale * total)[:, :64]
-    pout[1] = (old_im - scale * swap(total))[:, :64]
-    probe_copy = pltpu.make_async_copy(pout, probe_out, out_sem.at[5])
-    probe_copy.start()
-
-    for copy in gathers + reduces + probe_x + ray_moves:
-        copy.wait_send()
-    first_move.wait_send()
-    second_move.wait_send()
+        if (n + 1) % (WCH // OUTS) == 0:
+            part = pl.ds(n // (WCH // OUTS) * rows, rows)
+            for t in range(4):
+                copy = pltpu.make_async_copy(
+                    onew.reshape(4, 8, 64, 128).at[t, :, part, :],
+                    obj_out.at[:, part, pl.ds(t * 128, 128)],
+                    sem.at[3 + len(obj_copies)],
+                )
+                copy.start()
+                obj_copies.append(copy)
     wave_copy.wait()
+    probe_copy.wait()
     for copy in obj_copies:
         copy.wait()
-    probe_copy.wait()
 
 
 def shards(
@@ -575,34 +655,31 @@
     ray_tables,
     radon_weights,
 ):
-    column = lax.axis_index("pb")
-    own_blocks = 64 // PB
-    place = ray_tables * own_blocks + ray_blocks % own_blocks
-    owner = ray_blocks // own_blocks
-    own_lists = lax.dynamic_slice_in_dim(owner * KEYS + place, column * 2, 2, 1)
-    row_keys = own_lists.transpose(1, 0, 2).reshape(2 * AA, LIST)
-    col_keys = jnp.where(owner == column, place, -1).transpose(2, 1, 0).reshape(LIST, NB * AA)
-    any_spec = pl.BlockSpec(memory_space=pl.ANY)
     smem = pl.BlockSpec(memory_space=pltpu.SMEM)
     vmem = pltpu.VMEM
-    wave_next, probe_next, object_next = pl.pallas_call(
+    hbm_spec = pl.BlockSpec(memory_space=pltpu.HBM)
+    vmem_spec = pl.BlockSpec(memory_space=pltpu.VMEM)
+    kept = pl.pallas_call(
         kernel,
         out_shape=(
-            jax.ShapeDtypeStruct((256, 128), F32),
-            jax.ShapeDtypeStruct((2, 64, 64), F32),
-            jax.ShapeDtypeStruct((512, 512), F32),
+            pltpu.VMEM((4096, 768), BF16),
+            pltpu.VMEM((2048, 128), F32),
+            pltpu.VMEM((256, 128), F32),
+            pltpu.VMEM((64, 128), F32),
+            pltpu.VMEM((64, 768), BF16),
         ),
-        in_specs=[smem] * 3 + [any_spec] * 9,
-        out_specs=[any_spec] * 3,
+        in_specs=[smem] * 3 + [hbm_spec] * 9,
+        out_specs=[vmem_spec] * 5,
         scratch_shapes=[
-            vmem((2048, 128), F32),
-            vmem((4096, 768), BF16),
             vmem((1024, 128), F32),
             vmem((256, 128), F32),
-            vmem((POS, 32, 128), F32),
-            vmem((2, 64, 128), F32),
+            vmem((POS, 4096), F32),
+            vmem((POS * 32, 128), F32),
+            vmem((2, 64, 64), F32),
+            vmem((640, 256), F32),
             vmem((6, 256, 256), BF16),
-            vmem((128, LIST), jnp.int32),
+            vmem((LIST * NB, AA), jnp.int32),
+            vmem((LIST * NB, AA), jnp.int32),
             vmem((LIST, 512), jnp.int32),
             vmem((2048, 128), F32),
             vmem((384, 128), F32),
@@ -617,27 +694,28 @@
             vmem((1024, 128), F32),
             vmem((768, 128), F32),
             vmem((256, 128), F32),
-            vmem((AA * SLOT, 128), F32),
-            vmem((AA * SLOT, 128), F32),
-            vmem((AA * SLOT, 128), F32),
-            vmem((AA * SLOT, 128), F32),
+            vmem((8 * SLOT, 128), F32),
+            vmem((8 * SLOT, 128), F32),
+            vmem((8 * SLOT, 128), F32),
+            vmem((8 * SLOT, 128), F32),
             vmem((256, 128), F32),
+            vmem((256, 128), BF16),
+            vmem((256, 128), BF16),
+            vmem((256, 128), F32),
+            vmem((256, 128), BF16),
+            vmem((256, 128), BF16),
             vmem((512, 256), BF16),
             vmem((384, 128), F32),
-            vmem((2048, 128), F32),
             vmem((32, 128), F32),
-            vmem((64, 128), F32),
-            vmem((2, 64, 64), F32),
             pltpu.SemaphoreType.DMA((14,)),
             pltpu.SemaphoreType.DMA((WCH,)),
-            pltpu.SemaphoreType.DMA((6,)),
             pltpu.SemaphoreType.DMA((12,)),
             pltpu.SemaphoreType.DMA((12,)),
-            pltpu.SemaphoreType.DMA((4,)),
-            pltpu.SemaphoreType.DMA((4,)),
+            pltpu.SemaphoreType.DMA((6,)),
+            pltpu.SemaphoreType.DMA((6,)),
         ],
         compiler_params=pltpu.CompilerParams(
-            collective_id=0, has_side_effects=True, vmem_limit_bytes=48 * 1024 * 1024
+            collective_id=0, has_side_effects=True, vmem_limit_bytes=54 * 1024 * 1024
         ),
         name="admm",
     )(
@@ -648,12 +726,30 @@
         radon_weights,
         wave_field.reshape(256, 512),
         scaled_dual.reshape(256, 128),
-        intensity.reshape(POS, 32, 128),
-        jnp.concatenate([probe_field, probe_field], axis=2),
+        intensity.reshape(POS, 4096),
+        probe_field,
         tables,
-        row_keys,
-        col_keys,
+        ray_blocks.transpose(2, 1, 0).reshape(LIST * NB, AA),
+        ray_tables.transpose(2, 1, 0).reshape(LIST * NB, AA),
     )
+    wave_next, probe_next, object_next = pl.pallas_call(
+        tail,
+        out_shape=(
+            jax.ShapeDtypeStruct((256, 128), F32),
+            jax.ShapeDtypeStruct((2, 64, 64), F32),
+            jax.ShapeDtypeStruct((8, 64, 512), F32),
+        ),
+        in_specs=[hbm_spec] + [vmem_spec] * 5,
+        out_specs=[hbm_spec] * 3,
+        scratch_shapes=[
+            vmem((2048, 128), F32),
+            vmem((2, 64, 64), F32),
+            vmem((2, 64, 64), F32),
+            pltpu.SemaphoreType.DMA((3 + 4 * OUTS,)),
+        ],
+        compiler_params=pltpu.CompilerParams(vmem_limit_bytes=16 * 1024 * 1024),
+        name="tail",
+    )(probe_field, *kept)
     return (
         wave_next.reshape(1, 2, 128, 128),
         probe_next,

time: 58.2 us -> 47.9 us (0.82)
  local copies, waits for them, and re-layouts: 9.7 us -> 0.01 us
  other arithmetic: 1.89 us -> 0 us
  Pallas kernels: 45.5 us -> 47.1 us
    unnamed x18 -> x2, local copies, waits for them, and re-layouts: 9.52 us -> 0.01 us
    pallas_call x1 -> x2, Pallas kernels: 45.5 us -> 47.1 us  [the longest x1 42.8 us: shards(): pl.pallas_call(kernel, out_shape=(pltpu.VMEM((4096, 768), BF16), pltpu.VM...]
    concatenate x1 -> x0, other arithmetic: 1 us -> none  [shards(): jnp.concatenate([probe_field, probe_field], axis=2)]
    transpose x2 -> x0, other arithmetic: 0.9 us -> none  [the longest x1 0.88 us: shards(): jnp.where(owner == column, place, -1).transpose(2, 1, 0)]
where the time goes in v2:
time: 47.9 us; the launch traced here: 47.7 us
  Pallas kernels  47.1 us (98%)
  between operations  0.66 us (1%)
    pallas_call x1, Pallas kernels, shards(): pl.pallas_call(kernel, out_shape=(pltpu.VMEM((4096, 768), BF16), pltpu.VM...  42.8 us
    pallas_call x1, Pallas kernels, shards(): pl.pallas_call(tail, out_shape=(jax.ShapeDtypeStruct((256, 128), F32), ja...  4.24 us

profile of v2, /device:TPU:1, one launch (start us, length us, event | category | flops | bytes accessed | tf_op | source)
XLA Modules:
  0.0 47.7 jit_solution(16089343123474022692)
XLA Ops:
  0.6 0.0 copy-start
  0.6 42.8 %admm.1 = (bf16[4096,768]{1,0:T(8,128)(2,1)S(1)}, f32[2048,128]{1,0:T(8,128)S(1)}, f32[256,128]{1,0:T(8,128)S(1)}, f32[64,128]{1,0:T(8,128)S(1)}, bf16[64,768]{1,0:T(8,128)(2,1)S(1)}) custom-call(s32[1,16]{1,0:T(1,128)} %rows_ref.1, s32[1,16]{1,0:T(1,128)} %cols_ref.1, s32[1,16]{1,0:T(1,128)} %mask_ref.1, f32[512,512]{1,0:T(8,128)} %bitcast.12, ...), custom_call_target="tpu_custom_call" | custom-call | tf_op jit(solution)/shard_map/admm/pallas_call | solution.py:662
  43.5 0.0 copy-done
  43.5 4.2 %tail.1 = (f32[256,128]{1,0:T(8,128)}, f32[2,64,64]{2,1,0:T(8,128)}, f32[8,64,512]{2,1,0:T(8,128)}) custom-call(f32[2,64,64]{2,1,0:T(8,128)S(1)} %copy-done, bf16[4096,768]{1,0:T(8,128)(2,1)S(1)} %get-tuple-element.11.wts, f32[2048,128]{1,0:T(8,128)S(1)} %get-tuple-element.12.obj, f32[256,128]{1,0:T(8,128)S(1)} %get-tuple-element.13.wnext, ...), custom_call_target="tpu_custom_call" | custom-call | tf_op jit(solution)/shard_map/tail/pallas_call | solution.py:735
Async XLA Ops:
  0.6 42.9 %copy-start = (f32[2,64,64]{2,1,0:T(8,128)S(1)}, f32[2,64,64]{2,1,0:T(8,128)}, u32[]{:S(2)}) copy-start(f32[2,64,64]{2,1,0:T(8,128)} %probe_hbm.3) | copy-start | bytes 98308

commit v3 on v2

--- a/solution.py
+++ b/solution.py
@@ -21,10 +21,17 @@
 KEYS = 192
 LAYER = 8
 DEPTH = 8
-SLOT = 40
-SLOT2 = 32
+ROWS = 4
+CHIPS = 32
+SLOT1 = 16
+SLOT2 = 8
+OFFSETS = sorted(
+    [(dz, dy) for dz in range(DEPTH) for dy in range(ROWS) if dz + dy > 0],
+    key=lambda o: (-min(o[0], DEPTH - o[0]) - min(o[1], ROWS - o[1]), o),
+)
 WCH = 8
 WROWS = 4096 // WCH
+WIDE = 384
 OUTS = 4
 
 WAVE_STEP = 0.05
@@ -139,15 +146,15 @@
     acc,
     share,
     base,
-    send1,
-    mid1,
-    turn1,
+    loose1,
+    across1,
+    arrived1,
+    message1,
     recv1,
-    loose,
-    send2,
-    mid2,
     loose2,
-    turn2,
+    across2,
+    arrived2,
+    message2,
     recv2,
     rays,
     spread,
@@ -161,15 +168,15 @@
 ):
     me_a = lax.axis_index("aa")
     me_p = lax.axis_index("pb")
+    core = me_a % 2
+    chip = me_a // 2
     z_own = me_a // LAYER
-    m_own = me_a % LAYER
+    y_own = chip % ROWS
     z_base = z_own * LAYER
-
-    def layer_peer(step):
-        return z_base + lax.rem(m_own + step, LAYER)
-
-    def depth_peer(step):
-        return lax.rem(z_own + step, DEPTH) * LAYER + m_own
+    sibling = me_a + 1 - 2 * core
+
+    def chip_at(dz, dy):
+        return lax.rem(z_own + dz, DEPTH) * ROWS + lax.rem(y_own + dy, ROWS)
 
     def lanes(shape):
         return lax.broadcasted_iota(jnp.int32, shape, 1)
@@ -182,9 +189,12 @@
     ]
     wts_in = [
         pltpu.make_async_copy(
-            wts_hbm.at[pl.ds(c * WROWS, WROWS)], wts.at[pl.ds(c * WROWS, WROWS)], w_sem.at[c]
-        )
-        for c in range(WCH)
+            wts_hbm.at[pl.ds(c * 1024, 1024), pl.ds(h * WIDE, WIDE)],
+            wts.at[pl.ds(c * 1024, 1024), pl.ds(h * WIDE, WIDE)],
+            w_sem.at[h * 4 + c],
+        )
+        for h in range(2)
+        for c in range(4)
     ]
     wave_in = [
         pltpu.make_async_copy(
@@ -214,17 +224,16 @@
 
     barrier = pltpu.get_barrier_semaphore()
 
-    for step in range(1, LAYER):
-        for peer in (layer_peer(step), depth_peer(step)):
-            pl.semaphore_signal(
-                barrier, inc=1, device_id={"aa": peer}, device_id_type=pl.DeviceIdType.MESH
-            )
     for step in range(1, PB):
         pl.semaphore_signal(
             barrier,
             inc=1,
             device_id={"pb": lax.rem(me_p + step, PB)},
             device_id_type=pl.DeviceIdType.MESH,
+        )
+    for peer in [chip_at(dz, dy) * 2 + core for dz, dy in OFFSETS] + [sibling]:
+        pl.semaphore_signal(
+            barrier, inc=1, device_id={"aa": peer}, device_id_type=pl.DeviceIdType.MESH
         )
 
     others["blocks"].wait()
@@ -258,33 +267,7 @@
         return carry
 
     lax.fori_loop(0, 32, fold, 0, unroll=4)
-    products = jnp.zeros((64, 768), F32)
-    per = 32 // WCH
-    for c in range(WCH):
-        wts_in[c].wait()
-        part = jnp.concatenate(
-            [lhs[(c * per + n) * 64 : (c * per + n + 1) * 64, :] for n in range(per)], axis=1
-        ).astype(BF16)
-        products = products + dot(part, wts[c * WROWS : (c + 1) * WROWS, :])
-    for t in range(6):
-        ptile[t * 64 : (t + 1) * 64, :] = products[:, t * 128 : (t + 1) * 128]
     own_stk = pl.multiple_of(me_p * KEYS, KEYS)
-    for t in range(6):
-        lists = [[], []], [[], []]
-        for br in range(2):
-            part = [ptile[pl.ds(t * 64 + cz * 2 + br, 8, stride=8), :] for cz in range(ZC)]
-            for c in range(2):
-                even, odd = interleave(part[2 * c], part[2 * c + 1])
-                lists[0][c].append(even)
-                lists[1][c].append(odd)
-        for h in range(2):
-            for c in range(2):
-                stk[
-                    pl.ds(pl.multiple_of(own_stk + (2 * t + h) * 16, 16), 16),
-                    c * 128 : (c + 1) * 128,
-                ] = jnp.concatenate(lists[h][c], axis=0).astype(BF16)
-
-    pl.semaphore_wait(barrier, LAYER - 1 + DEPTH - 1 + PB - 1)
 
     def to_x(stage, step, src, dst):
         peer = lax.rem(me_p + step, PB)
@@ -297,25 +280,40 @@
             device_id_type=pl.DeviceIdType.MESH,
         )
 
-    own_block = stk.at[pl.ds(own_stk, KEYS)]
-    gathers = [to_x(0, step, own_block, own_block) for step in range(1, PB)]
-    for copy in gathers:
-        copy.start()
-
-    def scatter_rows(ref, slot, k, value):
-        for h in range(8):
-            ref[pl.ds(k * 8 + h, 8, stride=slot), :] = value[h * 8 : (h + 1) * 8]
-
-    def turn_rows(source, target, slot):
-        for h in range(8):
-            target[h * slot : h * slot + 32, :] = jnp.concatenate(
-                [source[pl.ds(k * 8 + h, 8, stride=slot), :] for k in range(4)], axis=0
-            ).astype(target.dtype)
-
-    def gather_rows(value, slot, k):
-        return jnp.concatenate(
-            [value[h * slot + k * 8 : h * slot + k * 8 + 8] for h in range(8)], axis=0
-        )
+    gathers = []
+    for half in range(2):
+        products = jnp.zeros((64, WIDE), F32)
+        for c in range(4):
+            wts_in[half * 4 + c].wait()
+            part = jnp.concatenate(
+                [lhs[(c * 8 + n) * 64 : (c * 8 + n + 1) * 64, :] for n in range(8)], axis=1
+            ).astype(BF16)
+            products = products + dot(
+                part, wts[c * 1024 : (c + 1) * 1024, half * WIDE : (half + 1) * WIDE]
+            )
+        for i in range(3):
+            t = half * 3 + i
+            ptile[t * 64 : (t + 1) * 64, :] = products[:, i * 128 : (i + 1) * 128]
+            lists = [[], []], [[], []]
+            for br in range(2):
+                part = [ptile[pl.ds(t * 64 + cz * 2 + br, 8, stride=8), :] for cz in range(ZC)]
+                for c in range(2):
+                    even, odd = interleave(part[2 * c], part[2 * c + 1])
+                    lists[0][c].append(even)
+                    lists[1][c].append(odd)
+            for h in range(2):
+                for c in range(2):
+                    stk[
+                        pl.ds(pl.multiple_of(own_stk + (2 * t + h) * 16, 16), 16),
+                        c * 128 : (c + 1) * 128,
+                    ] = jnp.concatenate(lists[h][c], axis=0).astype(BF16)
+        if half == 0:
+            pl.semaphore_wait(barrier, CHIPS + PB - 1)
+        own_block = stk.at[pl.ds(pl.multiple_of(own_stk + half * 96, 96), 96)]
+        for step in (2, 1, 3):
+            copy = to_x(4 * half, step, own_block, own_block)
+            copy.start()
+            gathers.append(copy)
 
     for copy in wave_in:
         copy.wait()
@@ -382,7 +380,7 @@
     grad_im = jnp.sum((w_re * back_im - w_im * back_re).reshape(PAIRS, 64, 128), axis=0)
     grad_re = grad_re + swap(grad_re)
     grad_im = grad_im + swap(grad_im)
-    scatter_rows(send1, SLOT, 4, jnp.where(lanes((64, 128)) < 64, grad_re, grad_im))
+    loose1[256:320, :] = jnp.where(lanes((64, 128)) < 64, grad_re, grad_im)
 
     pad[...] = jnp.zeros_like(pad)
     acc[...] = jnp.zeros_like(acc)
@@ -425,8 +423,8 @@
         first, second = interleave(
             projection[:64, c * 128 : (c + 1) * 128], projection[64:, c * 128 : (c + 1) * 128]
         )
-        scatter_rows(send1, SLOT, 2 * c, first)
-        scatter_rows(send1, SLOT, 2 * c + 1, second)
+        loose1[2 * c * 64 : 2 * c * 64 + 64, :] = first
+        loose1[2 * c * 64 + 64 : 2 * c * 64 + 128, :] = second
 
     def to_a(stage, peer, src, dst):
         return pltpu.make_async_remote_copy(
@@ -438,26 +436,45 @@
             device_id_type=pl.DeviceIdType.MESH,
         )
 
-    def exchange(stage, source, target, slot, count):
-        own = (m_own, z_own)[stage % 2]
-        for step in range(1, 8):
-            there = lax.rem(own + step, 8)
+    def exchange(stage, loose, across, arrived, message, target, slot, count):
+        rows = 160 if slot == SLOT1 else 128
+        for k in range(rows // 32):
+            across[k * 32 : k * 32 + 32, :] = loose[pl.ds(k * 64 + 1 - core, 32, stride=2), :]
+        swapped = to_a(stage, sibling, across.at[pl.ds(0, rows)], arrived.at[pl.ds(0, rows)])
+        swapped.start()
+        for k in range(4):
+            message[pl.ds(core * 4 + k, 32, stride=slot), :] = loose[
+                pl.ds(k * 64 + core, 32, stride=2), :
+            ]
+        swapped.wait_recv()
+        for k in range(4):
+            message[pl.ds((1 - core) * 4 + k, 32, stride=slot), :] = arrived[
+                k * 32 : k * 32 + 32, :
+            ]
+        if slot == SLOT1:
+            message[pl.ds(8, 32, stride=slot), :] = (
+                loose[pl.ds(256 + core, 32, stride=2), :] + arrived[128:160, :]
+            )
+        here = pl.ds(pl.multiple_of(chip * slot, 8), count)
+        for dz, dy in OFFSETS:
+            there = chip_at(dz, dy)
             to_a(
-                stage,
-                (layer_peer, depth_peer)[stage % 2](step),
-                source.at[pl.ds(pl.multiple_of(there * slot, 8), count)],
-                target.at[pl.ds(pl.multiple_of(own * slot, 8), count)],
+                stage + 1,
+                there * 2 + core,
+                message.at[pl.ds(pl.multiple_of(there * slot, 8), count)],
+                target.at[here],
             ).start()
-        here = pl.ds(pl.multiple_of(own * slot, 16 if slot == SLOT2 else 8), count)
-        target[here, :] = source[here, :]
-        return to_a(
-            stage,
-            (layer_peer, depth_peer)[stage % 2](1),
-            source.at[pl.ds(0, 7 * count)],
-            target.at[pl.ds(0, 7 * count)],
-        )
-
-    moves = [exchange(0, send1, mid1, SLOT, SLOT)]
+        target[here, :] = message[here, :]
+        rows = (CHIPS - 1) * count
+        moved = to_a(
+            stage + 1,
+            chip_at(0, 1) * 2 + core,
+            message.at[pl.ds(0, rows)],
+            target.at[pl.ds(0, rows)],
+        )
+        return [swapped, moved]
+
+    moves = exchange(0, loose1, across1, arrived1, message1, recv1, SLOT1, 9)
 
     for p in range(PB):
         parts = []
@@ -474,14 +491,6 @@
             total = total + jnp.where(colkey[e : e + 1, :] == mine, 1.0, 0.0)
         hit_c[r * 64 : (r + 1) * 64, :] = total.astype(BF16)
 
-    moves[0].wait_recv()
-    turn_rows(mid1, turn1, SLOT)
-    partial = mid1[32:40, :]
-    for l in range(1, 8):
-        partial = partial + mid1[l * SLOT + 32 : l * SLOT + 40, :]
-    turn1[pl.ds(32, 8, stride=SLOT), :] = partial
-    moves.append(exchange(1, turn1, recv1, SLOT, 33))
-
     others["dual"].wait()
     own_cols = pl.ds(pl.multiple_of(me_p * 256, 256), 256)
     mine = wave[own_cols, :]
@@ -491,43 +500,40 @@
     base[...] = mine - WAVE_STEP * (gradient + PENALTY * (mine + dual[...]))
 
     moves[1].wait_recv()
-    for c in range(2):
-        for z in range(2):
-            there = pl.ds(c * 128 + z, 64, stride=2)
-            here = gather_rows(recv1, SLOT, 2 * c + z)
-            moved = base[there, :] + (WAVE_STEP * PENALTY) * here
-            wnext[there, :] = moved
-            scatter_rows(loose, SLOT2, 2 * c + z, here - (moved + dual[there, :]))
-    send2[...] = loose[...].astype(BF16)
-    moves.append(exchange(2, send2, mid2, SLOT2, SLOT2))
+    for half in range(2):
+        for c in range(2):
+            for z in range(2):
+                k = 2 * c + z
+                there = pl.ds(c * 128 + 2 * half + z, 32, stride=4)
+                here = recv1[pl.ds(half * 4 + k, 32, stride=SLOT1), :]
+                moved = base[there, :] + (WAVE_STEP * PENALTY) * here
+                wnext[there, :] = moved
+                misfit = here - (moved + dual[there, :])
+                loose2[pl.ds(k * 64 + half, 32, stride=2), :] = misfit.astype(BF16).astype(F32)
+    moves += exchange(2, loose2, across2, arrived2, message2, recv2, SLOT2, 8)
 
     own_row = pl.ds(pl.multiple_of(me_p * 8, 8), 1)
-    prow[own_row, :] = jnp.sum(recv1[pl.ds(32, 8, stride=SLOT), :], axis=0, keepdims=True)
+    prow[own_row, :] = jnp.sum(recv1[pl.ds(8, 32, stride=SLOT1), :], axis=0, keepdims=True)
     probe_x = [to_x(3, step, prow.at[own_row], prow.at[own_row]) for step in range(1, PB)]
     for copy in probe_x:
         copy.start()
-    moves[2].wait_recv()
-    loose2[...] = mid2[...].astype(F32)
-    turn_rows(loose2, turn2, SLOT2)
-    moves.append(exchange(3, turn2, recv2, SLOT2, SLOT2))
-
     for copy in probe_x:
         copy.wait_recv()
     pfull[pl.ds(me_a, 1), :] = (prow[0:1, :] + prow[8:9, :]) + (prow[16:17, :] + prow[24:25, :])
 
-    def layer(step):
-        row = pfull.at[pl.ds(me_a, 1)]
-        return to_a(4, layer_peer(step), row, row)
-
-    for step in range(1, LAYER):
-        layer(step).start()
+    own_row = pfull.at[pl.ds(me_a, 1)]
+    probe_core = to_a(4, sibling, own_row, own_row)
+    probe_core.start()
+    probe_core.wait_recv()
+    two = pfull.at[pl.ds(chip * 2, 2)]
+    for step in range(1, ROWS):
+        to_a(5, chip_at(0, step) * 2 + core, two, two).start()
 
     moves[3].wait_recv()
     own_rays = pl.multiple_of(me_p * 128, 128)
-    arrived = recv2[...].astype(F32)
     for c in range(2):
         first, second = interleave(
-            gather_rows(arrived, SLOT2, 2 * c), gather_rows(arrived, SLOT2, 2 * c + 1)
+            recv2[pl.ds(2 * c, 64, stride=4), :], recv2[pl.ds(2 * c + 1, 64, stride=4), :]
         )
         rays[pl.ds(own_rays, 128), c * 128 : (c + 1) * 128] = jnp.concatenate(
             [first, second], axis=0
@@ -537,14 +543,13 @@
     for copy in ray_moves:
         copy.start()
 
-    seven = pfull.at[pl.ds(0, LAYER - 1)]
-    layer_all = to_a(4, layer_peer(1), seven, seven)
+    six = pfull.at[pl.ds(0, 6)]
+    layer_all = to_a(5, chip_at(0, 1) * 2 + core, six, six)
     layer_all.wait_recv()
-    layer_all.wait_send()
     group = pfull.at[pl.ds(pl.multiple_of(z_base, 8), 8)]
 
     def stack(step):
-        return to_a(5, depth_peer(step), group, group)
+        return to_a(6, chip_at(step, 0) * 2 + core, group, group)
 
     for step in range(1, DEPTH):
         stack(step).start()
@@ -568,12 +573,12 @@
     ).astype(BF16)
 
     others_all = pfull.at[pl.ds(0, 7 * LAYER)]
-    stack_all = to_a(5, depth_peer(1), others_all, others_all)
+    stack_all = to_a(6, chip_at(1, 0) * 2 + core, others_all, others_all)
     stack_all.wait_recv()
     stack_all.wait_send()
     for copy in gathers + reduces + probe_x + ray_moves:
         copy.wait_send()
-    for copy in moves:
+    for copy in moves + [probe_core, layer_all]:
         copy.wait_send()
 
 
@@ -694,25 +699,25 @@
             vmem((1024, 128), F32),
             vmem((768, 128), F32),
             vmem((256, 128), F32),
-            vmem((8 * SLOT, 128), F32),
-            vmem((8 * SLOT, 128), F32),
-            vmem((8 * SLOT, 128), F32),
-            vmem((8 * SLOT, 128), F32),
+            vmem((320, 128), F32),
+            vmem((160, 128), F32),
+            vmem((160, 128), F32),
+            vmem((CHIPS * SLOT1, 128), F32),
+            vmem((CHIPS * SLOT1, 128), F32),
             vmem((256, 128), F32),
-            vmem((256, 128), BF16),
-            vmem((256, 128), BF16),
-            vmem((256, 128), F32),
-            vmem((256, 128), BF16),
-            vmem((256, 128), BF16),
+            vmem((128, 128), F32),
+            vmem((128, 128), F32),
+            vmem((CHIPS * SLOT2, 128), F32),
+            vmem((CHIPS * SLOT2, 128), F32),
             vmem((512, 256), BF16),
             vmem((384, 128), F32),
             vmem((32, 128), F32),
             pltpu.SemaphoreType.DMA((14,)),
             pltpu.SemaphoreType.DMA((WCH,)),
-            pltpu.SemaphoreType.DMA((12,)),
-            pltpu.SemaphoreType.DMA((12,)),
-            pltpu.SemaphoreType.DMA((6,)),
-            pltpu.SemaphoreType.DMA((6,)),
+            pltpu.SemaphoreType.DMA((15,)),
+            pltpu.SemaphoreType.DMA((15,)),
+            pltpu.SemaphoreType.DMA((7,)),
+            pltpu.SemaphoreType.DMA((7,)),
         ],
         compiler_params=pltpu.CompilerParams(
             collective_id=0, has_side_effects=True, vmem_limit_bytes=54 * 1024 * 1024

time: 47.9 us -> 43.4 us (0.906)
  Pallas kernels: 47.1 us -> 42.6 us
    pallas_call x1, Pallas kernels: 42.8 us -> 38.4 us  [shards(): pl.pallas_call(kernel, out_shape=(pltpu.VMEM((4096, 768), BF16), pltpu.VM...]
where the time goes in v3:
time: 43.4 us; the launch traced here: 43.3 us
  Pallas kernels  42.6 us (98%)
  between operations  0.66 us (2%)
    pallas_call x1, Pallas kernels, shards(): pl.pallas_call(kernel, out_shape=(pltpu.VMEM((4096, 768), BF16), pltpu.VM...  38.4 us
    pallas_call x1, Pallas kernels, shards(): pl.pallas_call(tail, out_shape=(jax.ShapeDtypeStruct((256, 128), F32), ja...  4.24 us

profile of v3, /device:TPU:1, one launch (start us, length us, event | category | flops | bytes accessed | tf_op | source)
XLA Modules:
  0.0 43.3 jit_solution(11471219968380671986)
XLA Ops:
  0.6 0.0 copy-start
  0.6 38.4 %admm.1 = (bf16[4096,768]{1,0:T(8,128)(2,1)S(1)}, f32[2048,128]{1,0:T(8,128)S(1)}, f32[256,128]{1,0:T(8,128)S(1)}, f32[64,128]{1,0:T(8,128)S(1)}, bf16[64,768]{1,0:T(8,128)(2,1)S(1)}) custom-call(s32[1,16]{1,0:T(1,128)} %rows_ref.1, s32[1,16]{1,0:T(1,128)} %cols_ref.1, s32[1,16]{1,0:T(1,128)} %mask_ref.1, f32[512,512]{1,0:T(8,128)} %bitcast.12, ...), custom_call_target="tpu_custom_call" | custom-call | tf_op jit(solution)/shard_map/admm/pallas_call | solution.py:667
  39.0 0.0 copy-done
  39.0 4.2 %tail.1 = (f32[256,128]{1,0:T(8,128)}, f32[2,64,64]{2,1,0:T(8,128)}, f32[8,64,512]{2,1,0:T(8,128)}) custom-call(f32[2,64,64]{2,1,0:T(8,128)S(1)} %copy-done, bf16[4096,768]{1,0:T(8,128)(2,1)S(1)} %get-tuple-element.11.wts, f32[2048,128]{1,0:T(8,128)S(1)} %get-tuple-element.12.obj, f32[256,128]{1,0:T(8,128)S(1)} %get-tuple-element.13.wnext, ...), custom_call_target="tpu_custom_call" | custom-call | tf_op jit(solution)/shard_map/tail/pallas_call | solution.py:740
Async XLA Ops:
  0.6 38.4 %copy-start = (f32[2,64,64]{2,1,0:T(8,128)S(1)}, f32[2,64,64]{2,1,0:T(8,128)}, u32[]{:S(2)}) copy-start(f32[2,64,64]{2,1,0:T(8,128)} %probe_hbm.3) | copy-start | bytes 98308

commit v4 on v3

v4 whole, which is shorter than its diff:
```python
import math

import jax
import jax.numpy as jnp
import numpy as np
from jax import lax
from jax.experimental import pallas as pl
from jax.experimental.pallas import tpu as pltpu
from jax.sharding import PartitionSpec as P

BLK = 64
NW = 12
NB = 8
LIST = 12
AA = 64
PB = 4
ZC = 4
POS = 16
PAIRS = 8
OWN = 64 // PB
KEYS = 192
LAYER = 8
DEPTH = 8
ROWS = 4
CHIPS = 32
SLOT = 16
SHARE = 272
OFFSETS = sorted(
    [(dz, dy) for dz in range(DEPTH) for dy in range(ROWS) if dz + dy > 0],
    key=lambda o: (-min(o[0], DEPTH - o[0]) - min(o[1], ROWS - o[1]), o),
)
WCH = 8
WROWS = 4096 // WCH
WIDE = 384

WAVE_STEP = 0.05
PENALTY = 1.0
PROBE_STEP = 0.05
OBJECT_STEP = 1.0

F32 = jnp.float32
BF16 = jnp.bfloat16


def dft_constants():
    index = np.arange(BLK)
    phase = (index[:, None] * index[None, :]) % BLK
    angle = phase.astype(np.float64) * (-2.0 * math.pi / BLK)
    f_re, f_im = np.cos(angle) / math.sqrt(BLK), np.sin(angle) / math.sqrt(BLK)
    pair = np.eye(2)

    def right(re, im):
        dre, dim = np.kron(pair, re), np.kron(pair, im)
        return np.block([[dre, dim], [-dim, dre]])

    def left(re, im):
        return np.block([[re, -im], [im, re]])

    order = np.concatenate([np.arange(0, BLK, 2), np.arange(1, BLK, 2)])
    rights = [right(f_re, f_im), right(f_re, -f_im)]
    lefts = np.concatenate(
        [left(f_re[order, :], f_im[order, :]), left(f_re[:, order], -f_im[:, order])], axis=1
    )
    return np.concatenate(rights + [lefts], axis=0).astype(np.float32)


def halves(value):
    high = value.astype(BF16)
    low = (value - high.astype(F32)).astype(BF16)
    return high, low


def dot(lhs, rhs):
    return jnp.dot(lhs, rhs, preferred_element_type=F32)


def right_apply(re, im, g_hi, g_lo):
    high, low = halves(jnp.concatenate([re, im], axis=1))
    out = dot(high, g_hi) + dot(low, g_hi) + dot(high, g_lo)
    return out[:, :128], out[:, 128:]


def left_apply(re, im, table):
    high, low = halves(jnp.concatenate([re, im], axis=0))
    out = dot(table, jnp.concatenate([high, low], axis=0))
    out = out[:128] + out[128:]
    return out[:64], out[64:]


def rows_to_lanes(value):
    return jnp.concatenate([value[q * 64 : (q + 1) * 64] for q in range(PAIRS)], axis=1)


def lanes_to_rows(value):
    return jnp.concatenate([value[:, q * 128 : (q + 1) * 128] for q in range(PAIRS)], axis=0)


def swap(value):
    return pltpu.roll(value, 64, 1)


def interleave(first, second):
    low = lax.broadcasted_iota(jnp.int32, first.shape, 1) < 64
    return jnp.where(low, first, swap(second)), jnp.where(low, swap(first), second)


def kernel(
    rows_ref,
    cols_ref,
    mask_ref,
    obj_hbm,
    wts_hbm,
    wave_hbm,
    dual_hbm,
    int_hbm,
    probe_hbm,
    tab_hbm,
    blocks_hbm,
    tables_hbm,
    wnext,
    pnext,
    onew,
    wts,
    obj,
    wave,
    dual,
    int_raw,
    inten,
    probe,
    tab_raw,
    tab,
    blocks,
    tables,
    colkey,
    lhs,
    ptile,
    stk,
    hit_r,
    hit_c,
    win_r,
    win_i,
    gra_r,
    gra_i,
    pad,
    acc,
    share,
    base,
    loose1,
    across1,
    arrived1,
    message1,
    recv1,
    loose2,
    misfit,
    across2,
    arrived2,
    message2,
    recv2,
    rays,
    spread,
    prow,
    in_sem,
    w_sem,
    x_send,
    x_recv,
    a_send,
    a_recv,
):
    me_a = lax.axis_index("aa")
    me_p = lax.axis_index("pb")
    core = me_a % 2
    chip = me_a // 2
    z_own = me_a // LAYER
    y_own = chip % ROWS
    z_base = z_own * LAYER
    sibling = me_a + 1 - 2 * core

    def chip_at(dz, dy):
        return lax.rem(z_own + dz, DEPTH) * ROWS + lax.rem(y_own + dy, ROWS)

    def lanes(shape):
        return lax.broadcasted_iota(jnp.int32, shape, 1)

    obj_in = [
        pltpu.make_async_copy(
            obj_hbm.at[:, pl.ds(t * 128, 128)], obj.at[pl.ds(t * 512, 512)], in_sem.at[t]
        )
        for t in range(4)
    ]
    wts_in = [
        pltpu.make_async_copy(
            wts_hbm.at[pl.ds(c * 1024, 1024), pl.ds(h * WIDE, WIDE)],
            wts.at[pl.ds(c * 1024, 1024), pl.ds(h * WIDE, WIDE)],
            w_sem.at[h * 4 + c],
        )
        for h in range(2)
        for c in range(4)
    ]
    wave_in = [
        pltpu.make_async_copy(
            wave_hbm.at[:, pl.ds(t * 128, 128)], wave.at[pl.ds(t * 256, 256)], in_sem.at[4 + t]
        )
        for t in range(4)
    ]
    others = {
        name: pltpu.make_async_copy(src, dst, in_sem.at[8 + n])
        for n, (name, src, dst) in enumerate(
            [
                ("blocks", blocks_hbm, blocks),
                ("tables", tables_hbm, tables),
                ("probe", probe_hbm, probe),
                ("tab", tab_hbm, tab_raw),
                ("inten", int_hbm, int_raw),
                ("dual", dual_hbm, dual),
            ]
        )
    }
    for copy in wave_in:
        copy.start()
    for name in ("probe", "tab", "inten"):
        others[name].start()
    for copy in obj_in + wts_in:
        copy.start()
    for name in ("dual", "blocks", "tables"):
        others[name].start()

    barrier = pltpu.get_barrier_semaphore()

    for step in range(1, PB):
        pl.semaphore_signal(
            barrier,
            inc=1,
            device_id={"pb": lax.rem(me_p + step, PB)},
            device_id_type=pl.DeviceIdType.MESH,
        )
    for peer in [chip_at(dz, dy) * 2 + core for dz, dy in OFFSETS] + [sibling]:
        pl.semaphore_signal(
            barrier, inc=1, device_id={"aa": peer}, device_id_type=pl.DeviceIdType.MESH
        )

    for copy in wave_in:
        copy.wait()

    def windows(q, carry):
        at = pl.multiple_of(q * 64, 64)
        for c, ref in ((0, win_r), (1, win_i)):
            found = []
            for h in range(2):
                row = rows_ref[0, 2 * q + h]
                col = cols_ref[0, 2 * q + h]
                tile = col // 128
                off = col % 128
                near = wave[pl.ds(tile * 256 + c * 128 + row, 64), :]
                far = wave[pl.ds(jnp.minimum(tile + 1, 3) * 256 + c * 128 + row, 64), :]
                both = jnp.where(lanes((64, 128)) >= off, near, far)
                found.append(pltpu.roll(both, (128 + 64 * h - off) % 128, 1))
            ref[pl.ds(at, 64), :] = jnp.where(lanes((64, 128)) < 64, found[0], found[1])
        return carry

    lax.fori_loop(0, PAIRS, windows, 0)
    others["probe"].wait()
    others["tab"].wait()
    others["inten"].wait()
    for octet in range(2):
        for t in range(32):
            inten[pl.ds(octet * 256 + t, 8, stride=32), :] = int_raw[
                octet * 8 : octet * 8 + 8, t * 128 : (t + 1) * 128
            ]
    for n in range(2):
        tab[2 * n], tab[2 * n + 1] = halves(tab_raw[n * 256 : (n + 1) * 256, :])
        high, low = halves(tab_raw[512:640, n * 128 : (n + 1) * 128])
        tab[4 + n] = jnp.concatenate(
            [jnp.concatenate([high] * 2, axis=1), jnp.concatenate([low] * 2, axis=1)], axis=0
        )
    one_re = jnp.concatenate([probe[0]] * 2, axis=1)
    one_im = jnp.concatenate([probe[1]] * 2, axis=1)
    p_re = jnp.concatenate([one_re] * PAIRS, axis=0)
    p_im = jnp.concatenate([one_im] * PAIRS, axis=0)
    w_re, w_im = win_r[...], win_i[...]
    half_re, half_im = right_apply(
        p_re * w_re - p_im * w_im, p_re * w_im + p_im * w_re, tab[0], tab[1]
    )
    far_re, far_im = left_apply(rows_to_lanes(half_re), rows_to_lanes(half_im), tab[4])
    measured, live = [], []
    for q in range(PAIRS):
        even, odd = interleave(
            inten[2 * q * 32 : 2 * q * 32 + 32, :], inten[2 * q * 32 + 32 : 2 * q * 32 + 64, :]
        )
        measured.append(jnp.concatenate([even, odd], axis=0))
        live.append(
            jnp.where(
                lanes((1, 128)) < 64, mask_ref[0, 2 * q].astype(F32), mask_ref[0, 2 * q + 1].astype(F32)
            )
        )
    measured = jnp.concatenate(measured, axis=1)
    live = jnp.concatenate(live, axis=1)
    factor = live * (far_re * far_re + far_im * far_im - measured)
    half_re, half_im = left_apply(factor * far_re, factor * far_im, tab[5])
    back_re, back_im = right_apply(lanes_to_rows(half_re), lanes_to_rows(half_im), tab[2], tab[3])
    gra_r[...] = p_re * back_re + p_im * back_im
    gra_i[...] = p_re * back_im - p_im * back_re
    grad_re = jnp.sum((w_re * back_re + w_im * back_im).reshape(PAIRS, 64, 128), axis=0)
    grad_im = jnp.sum((w_re * back_im - w_im * back_re).reshape(PAIRS, 64, 128), axis=0)
    grad_re = grad_re + swap(grad_re)
    grad_im = grad_im + swap(grad_im)
    probe_part = jnp.where(lanes((64, 128)) < 64, grad_re, grad_im)

    pad[...] = jnp.zeros_like(pad)
    acc[...] = jnp.zeros_like(acc)
    for t in range(PB):
        acc[t * SHARE + 256 : (t + 1) * SHARE, :] = probe_part[t * 16 : (t + 1) * 16]

    def scatter(q, carry):
        at = pl.multiple_of(q * 64, 64)
        for h in range(2):
            row = rows_ref[0, 2 * q + h]
            col = cols_ref[0, 2 * q + h]
            turn = (col + 128 - 64 * h) % 128
            for c, ref in ((0, gra_r), (1, gra_i)):
                slot = (2 * h + c) * 192
                pad[slot + 64 : slot + 128, :] = pltpu.roll(ref[pl.ds(at, 64), :], turn, 1)
                moved = pad[pl.ds(slot + 64 - row, 128), :]
                for t in range(4):
                    place = lanes((128, 128)) + (t * 128 - col)
                    start = t * SHARE + c * 128
                    acc[start : start + 128, :] = acc[start : start + 128, :] + jnp.where(
                        (place >= 0) & (place < 64), moved, 0.0
                    )
        return carry

    lax.fori_loop(0, PAIRS, scatter, 0)
    def to_x(stage, step, src, dst):
        peer = lax.rem(me_p + step, PB)
        return pltpu.make_async_remote_copy(
            src_ref=src,
            dst_ref=dst,
            send_sem=x_send.at[stage * 3 + step - 1],
            recv_sem=x_recv.at[stage * 3 + step - 1],
            device_id={"pb": peer},
            device_id_type=pl.DeviceIdType.MESH,
        )

    pl.semaphore_wait(barrier, CHIPS + PB - 1)
    reduces = [
        to_x(
            0,
            step,
            acc.at[pl.ds(pl.multiple_of(lax.rem(me_p + step, PB) * SHARE, 16), SHARE)],
            share.at[pl.ds((step - 1) * SHARE, SHARE)],
        )
        for step in (2, 1, 3)
    ]
    for copy in reduces:
        copy.start()

    for copy in obj_in:
        copy.wait()

    def fold(q, carry):
        for t in range(4):
            even = obj[pl.ds(t * 512 + 2 * q, 8, stride=64), :]
            odd = obj[pl.ds(t * 512 + 2 * q + 1, 8, stride=64), :]
            first, second = interleave(even, odd)
            at = pl.multiple_of(q * 64 + t * 16, 16)
            lhs[pl.ds(at, 16), :] = jnp.concatenate([first, second], axis=0)
        return carry

    lax.fori_loop(0, 32, fold, 0, unroll=4)
    own_stk = pl.multiple_of(me_p * KEYS, KEYS)
    for half in range(2):
        products = jnp.zeros((64, WIDE), F32)
        for c in range(4):
            wts_in[half * 4 + c].wait()
            part = jnp.concatenate(
                [lhs[(c * 8 + n) * 64 : (c * 8 + n + 1) * 64, :] for n in range(8)], axis=1
            ).astype(BF16)
            products = products + dot(
                part, wts[c * 1024 : (c + 1) * 1024, half * WIDE : (half + 1) * WIDE]
            )
        for i in range(3):
            t = half * 3 + i
            ptile[t * 64 : (t + 1) * 64, :] = products[:, i * 128 : (i + 1) * 128]
            lists = [[], []], [[], []]
            for br in range(2):
                part = [ptile[pl.ds(t * 64 + cz * 2 + br, 8, stride=8), :] for cz in range(ZC)]
                for c in range(2):
                    even, odd = interleave(part[2 * c], part[2 * c + 1])
                    lists[0][c].append(even)
                    lists[1][c].append(odd)
            for h in range(2):
                for c in range(2):
                    stk[
                        pl.ds(pl.multiple_of(own_stk + (2 * t + h) * 16, 16), 16),
                        c * 128 : (c + 1) * 128,
                    ] = jnp.concatenate(lists[h][c], axis=0).astype(BF16)

    others["blocks"].wait()
    others["tables"].wait()
    keys = []
    for jj in range(2):
        there = pl.ds(me_p * 2 + jj, LIST, stride=NB)
        block = blocks[there, :]
        keys.append((block // OWN) * KEYS + tables[there, :] * OWN + block % OWN)
    keys = jnp.concatenate(
        [jnp.concatenate(keys, axis=1), jnp.zeros((128 - LIST, 128), jnp.int32)], axis=0
    )
    keys = jnp.transpose(keys.astype(F32)).astype(jnp.int32)
    for t in range(6):
        column = lanes((128, 128)) + t * 128
        total = jnp.zeros((128, 128), F32)
        for e in range(LIST):
            total = total + jnp.where(keys[:, e : e + 1] == column, 1.0, 0.0)
        hit_r[:, t * 128 : (t + 1) * 128] = total.astype(BF16)

    for p in range(PB):
        parts = []
        for jj in range(2):
            there = pl.ds(p * 2 + jj, LIST, stride=NB)
            block = blocks[there, :]
            place = tables[there, :] * OWN + block % OWN
            parts.append(jnp.where(block // OWN == me_p, place, -1))
        colkey[:, p * 128 : (p + 1) * 128] = jnp.concatenate(parts, axis=1)
    for r in range(3):
        mine = lax.broadcasted_iota(jnp.int32, (64, 512), 0) + r * 64
        total = jnp.zeros((64, 512), F32)
        for e in range(LIST):
            total = total + jnp.where(colkey[e : e + 1, :] == mine, 1.0, 0.0)
        hit_c[r * 64 : (r + 1) * 64, :] = total.astype(BF16)

    def to_a(stage, peer, src, dst):
        return pltpu.make_async_remote_copy(
            src_ref=src,
            dst_ref=dst,
            send_sem=a_send.at[stage],
            recv_sem=a_recv.at[stage],
            device_id={"aa": peer},
            device_id_type=pl.DeviceIdType.MESH,
        )

    def swap_cores(stage, loose, extra, across, arrived):
        for k in range(4):
            across[k * 32 : k * 32 + 32, :] = loose[pl.ds(k * 64 + 1 - core, 32, stride=2), :]
        if extra is not None:
            across[128:144, :] = extra
        rows = 128 if extra is None else 144
        copy = to_a(stage, sibling, across.at[pl.ds(0, rows)], arrived.at[pl.ds(0, rows)])
        copy.start()
        return copy

    def fill(loose, arrived, message):
        for k in range(4):
            message[pl.ds(core * 4 + k, 32, stride=SLOT), :] = loose[
                pl.ds(k * 64 + core, 32, stride=2), :
            ]
            message[pl.ds((1 - core) * 4 + k, 32, stride=SLOT), :] = arrived[
                k * 32 : k * 32 + 32, :
            ]

    def exchange(stage, message, target, count):
        here = pl.ds(pl.multiple_of(chip * SLOT, SLOT), count)
        for dz, dy in OFFSETS:
            there = chip_at(dz, dy)
            to_a(
                stage,
                there * 2 + core,
                message.at[pl.ds(pl.multiple_of(there * SLOT, SLOT), count)],
                target.at[here],
            ).start()
        target[here, :] = message[here, :]
        rows = (CHIPS - 1) * count
        return to_a(
            stage,
            chip_at(0, 1) * 2 + core,
            message.at[pl.ds(0, rows)],
            target.at[pl.ds(0, rows)],
        )

    others["dual"].wait()
    mine = wave[pl.ds(pl.multiple_of(me_p * 256, 256), 256), :]
    for copy in reduces:
        copy.wait_recv()
    own_share = pl.multiple_of(me_p * SHARE, 16)
    gradient = acc[pl.ds(own_share, 256), :]
    probe_share = acc[pl.ds(own_share + 256, 16), :]
    for n in range(PB - 1):
        gradient = gradient + share[n * SHARE : n * SHARE + 256, :]
        probe_share = probe_share + share[n * SHARE + 256 : (n + 1) * SHARE, :]
    base[...] = mine - WAVE_STEP * (gradient + PENALTY * (mine + dual[...]))
    for c in range(2):
        for z in range(2):
            there = pl.ds(c * 128 + z, 64, stride=2)
            k = 2 * c + z
            loose1[k * 64 : k * 64 + 64, :] = base[there, :] + dual[there, :]
    swap1 = swap_cores(0, loose1, probe_share, across1, arrived1)
    own_block = stk.at[pl.ds(own_stk, KEYS)]
    gathers = [to_x(1, step, own_block, own_block) for step in (2, 1, 3)]
    for copy in gathers:
        copy.start()
    swap1.wait_recv()
    fill(loose1, arrived1, message1)
    probe_chip = probe_share + arrived1[128:144, :]
    message1[pl.ds(8, 32, stride=SLOT), :] = jnp.concatenate([probe_chip] * 2, axis=0)
    move1 = exchange(1, message1, recv1, 9)

    for copy in gathers:
        copy.wait_recv()
    projection = dot(hit_r[...], stk[...])
    for c in range(2):
        first, second = interleave(
            projection[:64, c * 128 : (c + 1) * 128], projection[64:, c * 128 : (c + 1) * 128]
        )
        loose2[2 * c * 64 : 2 * c * 64 + 64, :] = first
        loose2[2 * c * 64 + 64 : 2 * c * 64 + 128, :] = second

    move1.wait_recv()
    for half in range(2):
        for k in range(4):
            there = pl.ds(k * 64 + half, 32, stride=2)
            own = loose2[there, :]
            rest = recv1[pl.ds(half * 4 + k, 32, stride=SLOT), :]
            misfit[there, :] = own - (rest + (WAVE_STEP * PENALTY) * own)
    own_rays = pl.multiple_of(me_p * 128, 128)
    for c in range(2):
        first, second = interleave(
            misfit[2 * c * 64 : 2 * c * 64 + 64, :], misfit[2 * c * 64 + 64 : 2 * c * 64 + 128, :]
        )
        rays[pl.ds(own_rays, 128), c * 128 : (c + 1) * 128] = jnp.concatenate(
            [first, second], axis=0
        ).astype(BF16)
    own_rows = rays.at[pl.ds(own_rays, 128)]
    ray_moves = [to_x(2, step, own_rows, own_rows) for step in (2, 1, 3)]
    for copy in ray_moves:
        copy.start()

    own_row = pl.ds(pl.multiple_of(me_p * 8, 8), 1)
    prow[own_row, :] = jnp.sum(recv1[pl.ds(8, 32, stride=SLOT), :], axis=0, keepdims=True)
    probe_x = [to_x(3, step, prow.at[own_row], prow.at[own_row]) for step in (2, 1, 3)]
    for copy in probe_x:
        copy.start()

    swap2 = swap_cores(2, loose2, None, across2, arrived2)
    swap2.wait_recv()
    fill(loose2, arrived2, message2)
    for copy in probe_x:
        copy.wait_recv()
    for p in range(PB):
        message2[pl.ds(8 + p, 32, stride=SLOT), :] = jnp.broadcast_to(
            prow[p * 8 : p * 8 + 1, :], (32, 128)
        )
    move2 = exchange(3, message2, recv2, 12)

    for copy in ray_moves:
        copy.wait_recv()

    sums = dot(hit_c[...], rays[...]).astype(BF16).astype(F32)
    for t in range(6):
        for br in range(2):
            for c in range(2):
                at = 2 * t * 16 + br * 8
                first, second = interleave(
                    sums[at : at + 8, c * 128 : (c + 1) * 128],
                    sums[at + 16 : at + 24, c * 128 : (c + 1) * 128],
                )
                spread[pl.ds(t * 64 + 4 * c + br, 8, stride=8), :] = first
                spread[pl.ds(t * 64 + 4 * c + 2 + br, 8, stride=8), :] = second
    table = jnp.concatenate(
        [spread[t * 64 : (t + 1) * 64, :] for t in range(6)], axis=1
    ).astype(BF16)

    for n in range(WCH):
        grad = lax.dot_general(
            table,
            wts[n * WROWS : (n + 1) * WROWS, :],
            (((1,), (1,)), ((), ())),
            preferred_element_type=F32,
        )
        per = 32 // WCH
        for s in range(per):
            q = n * per + s
            for t in range(4):
                first, second = interleave(
                    grad[t * 16 : t * 16 + 8, s * 128 : (s + 1) * 128],
                    grad[t * 16 + 8 : t * 16 + 16, s * 128 : (s + 1) * 128],
                )
                even = pl.ds(t * 512 + 2 * q, 8, stride=64)
                odd = pl.ds(t * 512 + 2 * q + 1, 8, stride=64)
                onew[even, :] = obj[even, :] - OBJECT_STEP * first
                onew[odd, :] = obj[odd, :] - OBJECT_STEP * second

    move2.wait_recv()
    for half in range(2):
        for c in range(2):
            for z in range(2):
                there = pl.ds(c * 128 + 2 * half + z, 32, stride=4)
                here = recv2[pl.ds(half * 4 + 2 * c + z, 32, stride=SLOT), :]
                wnext[there, :] = base[there, :] + (WAVE_STEP * PENALTY) * here
    total = jnp.concatenate(
        [recv2[pl.ds(8 + p, 16, stride=SLOT), :] for p in range(PB)], axis=0
    )
    scale = PROBE_STEP / (AA * POS * PB)
    pnext[0] = probe[0] - scale * total[:, :64]
    pnext[1] = probe[1] - scale * swap(total)[:, :64]

    for copy in gathers + reduces + probe_x + ray_moves + [swap1, move1, swap2, move2]:
        copy.wait_send()


def tail(wnext, pnext, onew, wave_out, probe_out, obj_out, sem):
    pairs = [
        (onew.at[pl.ds(t * 512, 512)], obj_out.at[:, pl.ds(t * 128, 128)]) for t in range(4)
    ] + [(wnext, wave_out), (pnext, probe_out)]
    copies = [pltpu.make_async_copy(src, dst, sem.at[n]) for n, (src, dst) in enumerate(pairs)]
    for copy in copies:
        copy.start()
    for copy in copies:
        copy.wait()


def shards(
    tables,
    wave_field,
    scaled_dual,
    intensity,
    probe_field,
    scan_rows,
    scan_cols,
    sample_mask,
    object_field,
    ray_blocks,
    ray_tables,
    radon_weights,
):
    smem = pl.BlockSpec(memory_space=pltpu.SMEM)
    vmem = pltpu.VMEM
    hbm_spec = pl.BlockSpec(memory_space=pltpu.HBM)
    vmem_spec = pl.BlockSpec(memory_space=pltpu.VMEM)
    kept = pl.pallas_call(
        kernel,
        out_shape=(
            pltpu.VMEM((256, 128), F32),
            pltpu.VMEM((2, 64, 64), F32),
            pltpu.VMEM((2048, 128), F32),
        ),
        in_specs=[smem] * 3 + [hbm_spec] * 9,
        out_specs=[vmem_spec] * 3,
        scratch_shapes=[
            vmem((4096, 768), BF16),
            vmem((2048, 128), F32),
            vmem((1024, 128), F32),
            vmem((256, 128), F32),
            vmem((POS, 4096), F32),
            vmem((POS * 32, 128), F32),
            vmem((2, 64, 64), F32),
            vmem((640, 256), F32),
            vmem((6, 256, 256), BF16),
            vmem((LIST * NB, AA), jnp.int32),
            vmem((LIST * NB, AA), jnp.int32),
            vmem((LIST, 512), jnp.int32),
            vmem((2048, 128), F32),
            vmem((384, 128), F32),
            vmem((768, 256), BF16),
            vmem((128, 768), BF16),
            vmem((KEYS, 512), BF16),
            vmem((512, 128), F32),
            vmem((512, 128), F32),
            vmem((512, 128), F32),
            vmem((512, 128), F32),
            vmem((768, 128), F32),
            vmem((PB * SHARE, 128), F32),
            vmem(((PB - 1) * SHARE, 128), F32),
            vmem((256, 128), F32),
            vmem((256, 128), F32),
            vmem((144, 128), F32),
            vmem((144, 128), F32),
            vmem((CHIPS * SLOT, 128), F32),
            vmem((CHIPS * SLOT, 128), F32),
            vmem((256, 128), F32),
            vmem((256, 128), F32),
            vmem((128, 128), F32),
            vmem((128, 128), F32),
            vmem((CHIPS * SLOT, 128), F32),
            vmem((CHIPS * SLOT, 128), F32),
            vmem((512, 256), BF16),
            vmem((384, 128), F32),
            vmem((32, 128), F32),
            pltpu.SemaphoreType.DMA((14,)),
            pltpu.SemaphoreType.DMA((WCH,)),
            pltpu.SemaphoreType.DMA((12,)),
            pltpu.SemaphoreType.DMA((12,)),
            pltpu.SemaphoreType.DMA((4,)),
            pltpu.SemaphoreType.DMA((4,)),
        ],
        compiler_params=pltpu.CompilerParams(
            collective_id=0, has_side_effects=True, vmem_limit_bytes=60 * 1024 * 1024
        ),
        name="admm",
    )(
        scan_rows,
        scan_cols,
        sample_mask,
        object_field.reshape(512, 512),
        radon_weights,
        wave_field.reshape(256, 512),
        scaled_dual.reshape(256, 128),
        intensity.reshape(POS, 4096),
        probe_field,
        tables,
        ray_blocks.transpose(2, 1, 0).reshape(LIST * NB, AA),
        ray_tables.transpose(2, 1, 0).reshape(LIST * NB, AA),
    )
    wave_next, probe_next, object_next = pl.pallas_call(
        tail,
        out_shape=(
            jax.ShapeDtypeStruct((256, 128), F32),
            jax.ShapeDtypeStruct((2, 64, 64), F32),
            jax.ShapeDtypeStruct((512, 512), F32),
        ),
        in_specs=[vmem_spec] * 3,
        out_specs=[hbm_spec] * 3,
        scratch_shapes=[pltpu.SemaphoreType.DMA((6,))],
        compiler_params=pltpu.CompilerParams(vmem_limit_bytes=16 * 1024 * 1024),
        name="tail",
    )(*kept)
    return (
        wave_next.reshape(1, 2, 128, 128),
        probe_next,
        object_next.reshape(2, 2, 128, 512),
    )


def solution(mesh):
    specs = (
        P("aa", None, None, None),
        P("aa", None, None, "pb"),
        P("aa", "pb", None),
        P(),
        P("aa", "pb"),
        P("aa", "pb"),
        P("aa", "pb"),
        P(None, "aa", "pb", None),
        P(),
        P(),
        P(),
    )
    mapped = jax.shard_map(
        shards,
        mesh=mesh,
        in_specs=(P(),) + specs,
        out_specs=(P("aa", None, None, "pb"), P(), P(None, "aa", "pb", None)),
        check_vma=False,
    )

    def step(*arrays):
        return mapped(jnp.asarray(dft_constants()), *arrays)

    return step
```

time: 43.4 us -> 42.2 us (0.972)
  Pallas kernels: 42.6 us -> 41.5 us
    pallas_call x1, Pallas kernels: 4.24 us -> 1.07 us  [shards(): pl.pallas_call(tail, out_shape=(jax.ShapeDtypeStruct((256, 128), F32), ja...]
    pallas_call x1, Pallas kernels: 38.4 us -> 40.4 us  [shards(): pl.pallas_call(kernel, out_shape=(pltpu.VMEM((256, 128), F32), pltpu.VMEM...]
where the time goes in v4:
time: 42.2 us; the launch traced here: 42.1 us
  Pallas kernels  41.5 us (98%)
  between operations  0.64 us (2%)
    pallas_call x1, Pallas kernels, shards(): pl.pallas_call(kernel, out_shape=(pltpu.VMEM((256, 128), F32), pltpu.VMEM...  40.4 us
    pallas_call x1, Pallas kernels, shards(): pl.pallas_call(tail, out_shape=(jax.ShapeDtypeStruct((256, 128), F32), ja...  1.07 us

profile of v4, /device:TPU:1, one launch (start us, length us, event | category | flops | bytes accessed | tf_op | source)
XLA Modules:
  0.0 42.1 jit_solution(5743181708572514244)
XLA Ops:
  0.6 40.4 %admm.1 = (f32[256,128]{1,0:T(8,128)S(1)}, f32[2,64,64]{2,1,0:T(8,128)S(1)}, f32[2048,128]{1,0:T(8,128)S(1)}) custom-call(s32[1,16]{1,0:T(1,128)} %rows_ref.1, s32[1,16]{1,0:T(1,128)} %cols_ref.1, s32[1,16]{1,0:T(1,128)} %mask_ref.1, f32[512,512]{1,0:T(8,128)} %bitcast.12, bf16[4096,768]{1,0:T(8,128)(2,1)} %wts_hbm.1, f32[256,512]{1,0:T(8,128)} %bitcast.13, ...), custom_call_target="tpu_custom_call" | custom-call | tf_op jit(solution)/shard_map/admm/pallas_call | solution.py:637
  41.0 1.1 %tail.1 = (f32[256,128]{1,0:T(8,128)}, f32[2,64,64]{2,1,0:T(8,128)}, f32[512,512]{1,0:T(8,128)}) custom-call(f32[256,128]{1,0:T(8,128)S(1)} %get-tuple-element.9.wnext, f32[2,64,64]{2,1,0:T(8,128)S(1)} %get-tuple-element.10.pnext, f32[2048,128]{1,0:T(8,128)S(1)} %get-tuple-element.11.onew), custom_call_target="tpu_custom_call" | custom-call | tf_op jit(solution)/shard_map/tail/pallas_call | solution.py:711

commit v5 on v4

--- a/solution.py
+++ b/solution.py
@@ -159,6 +159,8 @@
     rays,
     spread,
     prow,
+    pfull,
+    probe_part,
     in_sem,
     w_sem,
     x_send,
@@ -233,16 +235,24 @@
             device_id={"pb": lax.rem(me_p + step, PB)},
             device_id_type=pl.DeviceIdType.MESH,
         )
-    for peer in [chip_at(dz, dy) * 2 + core for dz, dy in OFFSETS] + [sibling]:
-        pl.semaphore_signal(
-            barrier, inc=1, device_id={"aa": peer}, device_id_type=pl.DeviceIdType.MESH
-        )
+    def clear(n, carry):
+        for at in (0, 128):
+            pad[pl.ds(pl.multiple_of(n * 192 + at, 64), 64), :] = jnp.zeros((64, 128), F32)
+        return carry
+
+    lax.fori_loop(0, 2 * POS, clear, 0)
 
     for copy in wave_in:
         copy.wait()
 
     def windows(q, carry):
         at = pl.multiple_of(q * 64, 64)
+        for n in range(CHIPS // PAIRS):
+            ahead = q * (CHIPS // PAIRS) + n
+            peer = jnp.where(ahead == 0, sibling, lax.rem(chip + ahead, CHIPS) * 2 + core)
+            pl.semaphore_signal(
+                barrier, inc=1, device_id={"aa": peer}, device_id_type=pl.DeviceIdType.MESH
+            )
         for c, ref in ((0, win_r), (1, win_i)):
             found = []
             for h in range(2):
@@ -303,32 +313,19 @@
     grad_im = jnp.sum((w_re * back_im - w_im * back_re).reshape(PAIRS, 64, 128), axis=0)
     grad_re = grad_re + swap(grad_re)
     grad_im = grad_im + swap(grad_im)
-    probe_part = jnp.where(lanes((64, 128)) < 64, grad_re, grad_im)
-
-    pad[...] = jnp.zeros_like(pad)
-    acc[...] = jnp.zeros_like(acc)
-    for t in range(PB):
-        acc[t * SHARE + 256 : (t + 1) * SHARE, :] = probe_part[t * 16 : (t + 1) * 16]
-
-    def scatter(q, carry):
+    probe_part[...] = jnp.where(lanes((64, 128)) < 64, grad_re, grad_im)
+
+    def place(q, carry):
         at = pl.multiple_of(q * 64, 64)
         for h in range(2):
-            row = rows_ref[0, 2 * q + h]
-            col = cols_ref[0, 2 * q + h]
-            turn = (col + 128 - 64 * h) % 128
+            turn = (cols_ref[0, 2 * q + h] + 128 - 64 * h) % 128
             for c, ref in ((0, gra_r), (1, gra_i)):
-                slot = (2 * h + c) * 192
-                pad[slot + 64 : slot + 128, :] = pltpu.roll(ref[pl.ds(at, 64), :], turn, 1)
-                moved = pad[pl.ds(slot + 64 - row, 128), :]
-                for t in range(4):
-                    place = lanes((128, 128)) + (t * 128 - col)
-                    start = t * SHARE + c * 128
-                    acc[start : start + 128, :] = acc[start : start + 128, :] + jnp.where(
-                        (place >= 0) & (place < 64), moved, 0.0
-                    )
+                slot = pl.multiple_of((4 * q + 2 * h + c) * 192 + 64, 64)
+                pad[pl.ds(slot, 64), :] = pltpu.roll(ref[pl.ds(at, 64), :], turn, 1)
         return carry
 
-    lax.fori_loop(0, PAIRS, scatter, 0)
+    lax.fori_loop(0, PAIRS, place, 0)
+
     def to_x(stage, step, src, dst):
         peer = lax.rem(me_p + step, PB)
         return pltpu.make_async_remote_copy(
@@ -341,17 +338,32 @@
         )
 
     pl.semaphore_wait(barrier, CHIPS + PB - 1)
-    reduces = [
-        to_x(
-            0,
-            step,
-            acc.at[pl.ds(pl.multiple_of(lax.rem(me_p + step, PB) * SHARE, 16), SHARE)],
-            share.at[pl.ds((step - 1) * SHARE, SHARE)],
-        )
-        for step in (2, 1, 3)
-    ]
-    for copy in reduces:
-        copy.start()
+    reduces = []
+    for step in (2, 1, 3, 0):
+        tile = lax.rem(me_p + step, PB)
+        for c in range(2):
+
+            def add(n, total, c=c, tile=tile):
+                moved = pad[pl.ds((2 * n + c) * 192 + 64 - rows_ref[0, n], 128), :]
+                column = lanes((128, 128)) + (tile * 128 - cols_ref[0, n])
+                return total + jnp.where((column >= 0) & (column < 64), moved, 0.0)
+
+            at = step * SHARE + c * 128
+            acc[at : at + 128, :] = lax.fori_loop(
+                0, POS, add, jnp.zeros((128, 128), F32), unroll=4
+            )
+        acc[step * SHARE + 256 : (step + 1) * SHARE, :] = probe_part[
+            pl.ds(pl.multiple_of(tile * 16, 16), 16), :
+        ]
+        if step > 0:
+            copy = to_x(
+                0,
+                step,
+                acc.at[pl.ds(step * SHARE, SHARE)],
+                share.at[pl.ds((step - 1) * SHARE, SHARE)],
+            )
+            copy.start()
+            reduces.append(copy)
 
     for copy in obj_in:
         copy.wait()
@@ -479,9 +491,8 @@
     mine = wave[pl.ds(pl.multiple_of(me_p * 256, 256), 256), :]
     for copy in reduces:
         copy.wait_recv()
-    own_share = pl.multiple_of(me_p * SHARE, 16)
-    gradient = acc[pl.ds(own_share, 256), :]
-    probe_share = acc[pl.ds(own_share + 256, 16), :]
+    gradient = acc[:256, :]
+    probe_share = acc[256:SHARE, :]
     for n in range(PB - 1):
         gradient = gradient + share[n * SHARE : n * SHARE + 256, :]
         probe_share = probe_share + share[n * SHARE + 256 : (n + 1) * SHARE, :]
@@ -512,6 +523,10 @@
         loose2[2 * c * 64 : 2 * c * 64 + 64, :] = first
         loose2[2 * c * 64 + 64 : 2 * c * 64 + 128, :] = second
 
+    swap2 = swap_cores(2, loose2, None, across2, arrived2)
+    swap2.wait_recv()
+    fill(loose2, arrived2, message2)
+
     move1.wait_recv()
     for half in range(2):
         for k in range(4):
@@ -538,16 +553,20 @@
     for copy in probe_x:
         copy.start()
 
-    swap2 = swap_cores(2, loose2, None, across2, arrived2)
-    swap2.wait_recv()
-    fill(loose2, arrived2, message2)
+    move2 = exchange(3, message2, recv2, 8)
+
     for copy in probe_x:
         copy.wait_recv()
-    for p in range(PB):
-        message2[pl.ds(8 + p, 32, stride=SLOT), :] = jnp.broadcast_to(
-            prow[p * 8 : p * 8 + 1, :], (32, 128)
-        )
-    move2 = exchange(3, message2, recv2, 12)
+    kind = chip % 16
+    own_four = pl.ds(pl.multiple_of(kind * 8, 8), 4)
+    pfull[own_four, :] = jnp.concatenate([prow[p * 8 : p * 8 + 1, :] for p in range(PB)], axis=0)
+
+    def share_rows(step):
+        four = pfull.at[own_four]
+        return to_a(4, (chip - kind + lax.rem(kind + step, 16)) * 2 + core, four, four)
+
+    for step in range(1, 16):
+        share_rows(step).start()
 
     for copy in ray_moves:
         copy.wait_recv()
@@ -594,14 +613,15 @@
                 there = pl.ds(c * 128 + 2 * half + z, 32, stride=4)
                 here = recv2[pl.ds(half * 4 + 2 * c + z, 32, stride=SLOT), :]
                 wnext[there, :] = base[there, :] + (WAVE_STEP * PENALTY) * here
-    total = jnp.concatenate(
-        [recv2[pl.ds(8 + p, 16, stride=SLOT), :] for p in range(PB)], axis=0
-    )
+    sixty = pfull.at[pl.ds(0, 60)]
+    probe_all = to_a(4, (chip - kind + lax.rem(kind + 1, 16)) * 2 + core, sixty, sixty)
+    probe_all.wait_recv()
+    total = jnp.concatenate([pfull[pl.ds(p, 16, stride=8), :] for p in range(PB)], axis=0)
     scale = PROBE_STEP / (AA * POS * PB)
     pnext[0] = probe[0] - scale * total[:, :64]
     pnext[1] = probe[1] - scale * swap(total)[:, :64]
 
-    for copy in gathers + reduces + probe_x + ray_moves + [swap1, move1, swap2, move2]:
+    for copy in gathers + reduces + probe_x + ray_moves + [swap1, move1, swap2, move2, probe_all]:
         copy.wait_send()
 
 
@@ -665,7 +685,7 @@
             vmem((512, 128), F32),
             vmem((512, 128), F32),
             vmem((512, 128), F32),
-            vmem((768, 128), F32),
+            vmem((2 * POS * 192, 128), F32),
             vmem((PB * SHARE, 128), F32),
             vmem(((PB - 1) * SHARE, 128), F32),
             vmem((256, 128), F32),
@@ -683,12 +703,14 @@
             vmem((512, 256), BF16),
             vmem((384, 128), F32),
             vmem((32, 128), F32),
+            vmem((128, 128), F32),
+            vmem((64, 128), F32),
             pltpu.SemaphoreType.DMA((14,)),
             pltpu.SemaphoreType.DMA((WCH,)),
             pltpu.SemaphoreType.DMA((12,)),
             pltpu.SemaphoreType.DMA((12,)),
-            pltpu.SemaphoreType.DMA((4,)),
-            pltpu.SemaphoreType.DMA((4,)),
+            pltpu.SemaphoreType.DMA((5,)),
+            pltpu.SemaphoreType.DMA((5,)),
         ],
         compiler_params=pltpu.CompilerParams(
             collective_id=0, has_side_effects=True, vmem_limit_bytes=60 * 1024 * 1024

time: 42.2 us -> 41.3 us (0.979)
  Pallas kernels: 41.5 us -> 40.4 us
    pallas_call x1, Pallas kernels: 40.4 us -> 39.3 us  [shards(): pl.pallas_call(kernel, out_shape=(pltpu.VMEM((256, 128), F32), pltpu.VMEM...]
where the time goes in v5:
time: 41.3 us; the launch traced here: 41 us
  Pallas kernels  40.4 us (98%)
  between operations  0.64 us (2%)
    pallas_call x1, Pallas kernels, shards(): pl.pallas_call(kernel, out_shape=(pltpu.VMEM((256, 128), F32), pltpu.VMEM...  39.3 us
    pallas_call x1, Pallas kernels, shards(): pl.pallas_call(tail, out_shape=(jax.ShapeDtypeStruct((256, 128), F32), ja...  1.07 us

profile of v5, /device:TPU:1, one launch (start us, length us, event | category | flops | bytes accessed | tf_op | source)
XLA Modules:
  0.0 41.0 jit_solution(4364260890829330835)
XLA Ops:
  0.6 39.3 %admm.1 = (f32[256,128]{1,0:T(8,128)S(1)}, f32[2,64,64]{2,1,0:T(8,128)S(1)}, f32[2048,128]{1,0:T(8,128)S(1)}) custom-call(s32[1,16]{1,0:T(1,128)} %rows_ref.1, s32[1,16]{1,0:T(1,128)} %cols_ref.1, s32[1,16]{1,0:T(1,128)} %mask_ref.1, f32[512,512]{1,0:T(8,128)} %bitcast.12, bf16[4096,768]{1,0:T(8,128)(2,1)} %wts_hbm.1, f32[256,512]{1,0:T(8,128)} %bitcast.13, ...), custom_call_target="tpu_custom_call" | custom-call | tf_op jit(solution)/shard_map/admm/pallas_call | solution.py:657
  39.9 1.1 %tail.1 = (f32[256,128]{1,0:T(8,128)}, f32[2,64,64]{2,1,0:T(8,128)}, f32[512,512]{1,0:T(8,128)}) custom-call(f32[256,128]{1,0:T(8,128)S(1)} %get-tuple-element.9.wnext, f32[2,64,64]{2,1,0:T(8,128)S(1)} %get-tuple-element.10.pnext, f32[2048,128]{1,0:T(8,128)S(1)} %get-tuple-element.11.onew), custom_call_target="tpu_custom_call" | custom-call | tf_op jit(solution)/shard_map/tail/pallas_call | solution.py:733

commit v6 on v5

--- a/solution.py
+++ b/solution.py
@@ -19,16 +19,10 @@
 PAIRS = 8
 OWN = 64 // PB
 KEYS = 192
-LAYER = 8
-DEPTH = 8
-ROWS = 4
 CHIPS = 32
 SLOT = 16
 SHARE = 272
-OFFSETS = sorted(
-    [(dz, dy) for dz in range(DEPTH) for dy in range(ROWS) if dz + dy > 0],
-    key=lambda o: (-min(o[0], DEPTH - o[0]) - min(o[1], ROWS - o[1]), o),
-)
+FIRST = 144
 WCH = 8
 WROWS = 4096 // WCH
 WIDE = 384
@@ -172,13 +166,7 @@
     me_p = lax.axis_index("pb")
     core = me_a % 2
     chip = me_a // 2
-    z_own = me_a // LAYER
-    y_own = chip % ROWS
-    z_base = z_own * LAYER
     sibling = me_a + 1 - 2 * core
-
-    def chip_at(dz, dy):
-        return lax.rem(z_own + dz, DEPTH) * ROWS + lax.rem(y_own + dy, ROWS)
 
     def lanes(shape):
         return lax.broadcasted_iota(jnp.int32, shape, 1)
@@ -221,11 +209,6 @@
         copy.start()
     for name in ("probe", "tab", "inten"):
         others[name].start()
-    for copy in obj_in + wts_in:
-        copy.start()
-    for name in ("dual", "blocks", "tables"):
-        others[name].start()
-
     barrier = pltpu.get_barrier_semaphore()
 
     for step in range(1, PB):
@@ -235,6 +218,15 @@
             device_id={"pb": lax.rem(me_p + step, PB)},
             device_id_type=pl.DeviceIdType.MESH,
         )
+    for peer in [lax.rem(chip + step, CHIPS) * 2 + core for step in range(1, CHIPS)] + [sibling]:
+        pl.semaphore_signal(
+            barrier, inc=1, device_id={"aa": peer}, device_id_type=pl.DeviceIdType.MESH
+        )
+    for copy in obj_in + wts_in:
+        copy.start()
+    for name in ("dual", "blocks", "tables"):
+        others[name].start()
+
     def clear(n, carry):
         for at in (0, 128):
             pad[pl.ds(pl.multiple_of(n * 192 + at, 64), 64), :] = jnp.zeros((64, 128), F32)
@@ -247,12 +239,6 @@
 
     def windows(q, carry):
         at = pl.multiple_of(q * 64, 64)
-        for n in range(CHIPS // PAIRS):
-            ahead = q * (CHIPS // PAIRS) + n
-            peer = jnp.where(ahead == 0, sibling, lax.rem(chip + ahead, CHIPS) * 2 + core)
-            pl.semaphore_signal(
-                barrier, inc=1, device_id={"aa": peer}, device_id_type=pl.DeviceIdType.MESH
-            )
         for c, ref in ((0, win_r), (1, win_i)):
             found = []
             for h in range(2):
@@ -338,32 +324,36 @@
         )
 
     pl.semaphore_wait(barrier, CHIPS + PB - 1)
-    reduces = []
-    for step in (2, 1, 3, 0):
-        tile = lax.rem(me_p + step, PB)
-        for c in range(2):
-
-            def add(n, total, c=c, tile=tile):
-                moved = pad[pl.ds((2 * n + c) * 192 + 64 - rows_ref[0, n], 128), :]
-                column = lanes((128, 128)) + (tile * 128 - cols_ref[0, n])
-                return total + jnp.where((column >= 0) & (column < 64), moved, 0.0)
-
-            at = step * SHARE + c * 128
-            acc[at : at + 128, :] = lax.fori_loop(
-                0, POS, add, jnp.zeros((128, 128), F32), unroll=4
-            )
-        acc[step * SHARE + 256 : (step + 1) * SHARE, :] = probe_part[
-            pl.ds(pl.multiple_of(tile * 16, 16), 16), :
-        ]
-        if step > 0:
-            copy = to_x(
-                0,
-                step,
-                acc.at[pl.ds(step * SHARE, SHARE)],
-                share.at[pl.ds((step - 1) * SHARE, SHARE)],
-            )
-            copy.start()
-            reduces.append(copy)
+    reduces = [[], []]
+    for half in range(2):
+        for step in (2, 1, 3, 0):
+            tile = lax.rem(me_p + step, PB)
+            at = step * SHARE + half * FIRST
+            for c in range(2):
+
+                def add(n, total, c=c, tile=tile, half=half):
+                    top = (2 * n + c) * 192 + 64 + half * 64 - rows_ref[0, n]
+                    column = lanes((64, 128)) + (tile * 128 - cols_ref[0, n])
+                    inside = (column >= 0) & (column < 64)
+                    return total + jnp.where(inside, pad[pl.ds(top, 64), :], 0.0)
+
+                acc[at + c * 64 : at + c * 64 + 64, :] = lax.fori_loop(
+                    0, POS, add, jnp.zeros((64, 128), F32), unroll=8
+                )
+            if half == 0:
+                acc[at + 128 : at + FIRST, :] = probe_part[
+                    pl.ds(pl.multiple_of(tile * 16, 16), 16), :
+                ]
+            if step > 0:
+                rows = FIRST if half == 0 else SHARE - FIRST
+                copy = to_x(
+                    half,
+                    step,
+                    acc.at[pl.ds(at, rows)],
+                    share.at[pl.ds((step - 1) * SHARE + half * FIRST, rows)],
+                )
+                copy.start()
+                reduces[half].append(copy)
 
     for copy in obj_in:
         copy.wait()
@@ -406,6 +396,11 @@
                         c * 128 : (c + 1) * 128,
                     ] = jnp.concatenate(lists[h][c], axis=0).astype(BF16)
 
+    own_block = stk.at[pl.ds(own_stk, KEYS)]
+    gathers = [to_x(2, step, own_block, own_block) for step in (2, 1, 3)]
+    for copy in gathers:
+        copy.start()
+
     others["blocks"].wait()
     others["tables"].wait()
     keys = []
@@ -449,69 +444,90 @@
             device_id_type=pl.DeviceIdType.MESH,
         )
 
-    def swap_cores(stage, loose, extra, across, arrived):
+    def swap_cores(stage, half, loose, extra, across, arrived):
+        at = half * 80
         for k in range(4):
-            across[k * 32 : k * 32 + 32, :] = loose[pl.ds(k * 64 + 1 - core, 32, stride=2), :]
+            across[at + k * 16 : at + k * 16 + 16, :] = loose[
+                pl.ds(k * 64 + half * 32 + 1 - core, 16, stride=2), :
+            ]
+        rows = 64
         if extra is not None:
-            across[128:144, :] = extra
-        rows = 128 if extra is None else 144
-        copy = to_a(stage, sibling, across.at[pl.ds(0, rows)], arrived.at[pl.ds(0, rows)])
+            across[64:80, :] = extra
+            rows = 80
+        copy = to_a(stage, sibling, across.at[pl.ds(at, rows)], arrived.at[pl.ds(at, rows)])
         copy.start()
         return copy
 
-    def fill(loose, arrived, message):
+    def fill(half, loose, arrived, message):
         for k in range(4):
-            message[pl.ds(core * 4 + k, 32, stride=SLOT), :] = loose[
-                pl.ds(k * 64 + core, 32, stride=2), :
+            message[pl.ds(half * 256 + core * 4 + k, 16, stride=SLOT), :] = loose[
+                pl.ds(k * 64 + half * 32 + core, 16, stride=2), :
             ]
-            message[pl.ds((1 - core) * 4 + k, 32, stride=SLOT), :] = arrived[
-                k * 32 : k * 32 + 32, :
+            message[pl.ds(half * 256 + (1 - core) * 4 + k, 16, stride=SLOT), :] = arrived[
+                half * 80 + k * 16 : half * 80 + k * 16 + 16, :
             ]
 
-    def exchange(stage, message, target, count):
+    def exchange(stage, half, message, target, count):
         here = pl.ds(pl.multiple_of(chip * SLOT, SLOT), count)
-        for dz, dy in OFFSETS:
-            there = chip_at(dz, dy)
+
+        def send(step):
+            there = half * 16 + lax.rem(chip + step, 16)
             to_a(
                 stage,
                 there * 2 + core,
                 message.at[pl.ds(pl.multiple_of(there * SLOT, SLOT), count)],
                 target.at[here],
             ).start()
-        target[here, :] = message[here, :]
+
+        for step in range(1, 16):
+            send(step)
+        pl.when(chip // 16 != half)(lambda: send(0))
+
+        @pl.when(chip // 16 == half)
+        def _():
+            target[here, :] = message[here, :]
+
         rows = (CHIPS - 1) * count
         return to_a(
             stage,
-            chip_at(0, 1) * 2 + core,
+            lax.rem(chip + 1, CHIPS) * 2 + core,
             message.at[pl.ds(0, rows)],
             target.at[pl.ds(0, rows)],
         )
 
     others["dual"].wait()
-    mine = wave[pl.ds(pl.multiple_of(me_p * 256, 256), 256), :]
-    for copy in reduces:
-        copy.wait_recv()
-    gradient = acc[:256, :]
-    probe_share = acc[256:SHARE, :]
-    for n in range(PB - 1):
-        gradient = gradient + share[n * SHARE : n * SHARE + 256, :]
-        probe_share = probe_share + share[n * SHARE + 256 : (n + 1) * SHARE, :]
-    base[...] = mine - WAVE_STEP * (gradient + PENALTY * (mine + dual[...]))
-    for c in range(2):
-        for z in range(2):
-            there = pl.ds(c * 128 + z, 64, stride=2)
-            k = 2 * c + z
-            loose1[k * 64 : k * 64 + 64, :] = base[there, :] + dual[there, :]
-    swap1 = swap_cores(0, loose1, probe_share, across1, arrived1)
-    own_block = stk.at[pl.ds(own_stk, KEYS)]
-    gathers = [to_x(1, step, own_block, own_block) for step in (2, 1, 3)]
-    for copy in gathers:
-        copy.start()
-    swap1.wait_recv()
-    fill(loose1, arrived1, message1)
-    probe_chip = probe_share + arrived1[128:144, :]
-    message1[pl.ds(8, 32, stride=SLOT), :] = jnp.concatenate([probe_chip] * 2, axis=0)
-    move1 = exchange(1, message1, recv1, 9)
+    swaps = []
+    for half in range(2):
+        for copy in reduces[half]:
+            copy.wait_recv()
+        for c in range(2):
+            at = half * FIRST + c * 64
+            gradient = acc[at : at + 64, :]
+            for n in range(PB - 1):
+                gradient = gradient + share[n * SHARE + at : n * SHARE + at + 64, :]
+            top = c * 128 + half * 64
+            mine = wave[pl.ds(pl.multiple_of(me_p * 256 + top, 64), 64), :]
+            base[top : top + 64, :] = mine - WAVE_STEP * (
+                gradient + PENALTY * (mine + dual[top : top + 64, :])
+            )
+            for z in range(2):
+                there = pl.ds(top + z, 32, stride=2)
+                k = 2 * c + z
+                loose1[k * 64 + half * 32 : k * 64 + half * 32 + 32, :] = (
+                    base[there, :] + dual[there, :]
+                )
+        probe_share = None
+        if half == 0:
+            probe_share = acc[128:FIRST, :]
+            for n in range(PB - 1):
+                probe_share = probe_share + share[n * SHARE + 128 : n * SHARE + FIRST, :]
+        swaps.append(swap_cores(half, half, loose1, probe_share, across1, arrived1))
+        swaps[-1].wait_recv()
+        fill(half, loose1, arrived1, message1)
+        if half == 0:
+            probe_chip = probe_share + arrived1[64:80, :]
+            message1[pl.ds(8, 32, stride=SLOT), :] = jnp.concatenate([probe_chip] * 2, axis=0)
+        move1 = exchange(2, half, message1, recv1, 9)
 
     for copy in gathers:
         copy.wait_recv()
@@ -523,9 +539,11 @@
         loose2[2 * c * 64 : 2 * c * 64 + 64, :] = first
         loose2[2 * c * 64 + 64 : 2 * c * 64 + 128, :] = second
 
-    swap2 = swap_cores(2, loose2, None, across2, arrived2)
-    swap2.wait_recv()
-    fill(loose2, arrived2, message2)
+    later = [swap_cores(3 + half, half, loose2, None, across2, arrived2) for half in range(2)]
+    for half in range(2):
+        later[half].wait_recv()
+        fill(half, loose2, arrived2, message2)
+    swaps += later
 
     move1.wait_recv()
     for half in range(2):
@@ -543,17 +561,18 @@
             [first, second], axis=0
         ).astype(BF16)
     own_rows = rays.at[pl.ds(own_rays, 128)]
-    ray_moves = [to_x(2, step, own_rows, own_rows) for step in (2, 1, 3)]
+    ray_moves = [to_x(3, step, own_rows, own_rows) for step in (2, 1, 3)]
     for copy in ray_moves:
         copy.start()
 
     own_row = pl.ds(pl.multiple_of(me_p * 8, 8), 1)
     prow[own_row, :] = jnp.sum(recv1[pl.ds(8, 32, stride=SLOT), :], axis=0, keepdims=True)
-    probe_x = [to_x(3, step, prow.at[own_row], prow.at[own_row]) for step in (2, 1, 3)]
+    probe_x = [to_x(4, step, prow.at[own_row], prow.at[own_row]) for step in (2, 1, 3)]
     for copy in probe_x:
         copy.start()
 
-    move2 = exchange(3, message2, recv2, 8)
+    for half in range(2):
+        move2 = exchange(5, half, message2, recv2, 8)
 
     for copy in probe_x:
         copy.wait_recv()
@@ -563,7 +582,7 @@
 
     def share_rows(step):
         four = pfull.at[own_four]
-        return to_a(4, (chip - kind + lax.rem(kind + step, 16)) * 2 + core, four, four)
+        return to_a(6, (chip - kind + lax.rem(kind + step, 16)) * 2 + core, four, four)
 
     for step in range(1, 16):
         share_rows(step).start()
@@ -614,14 +633,15 @@
                 here = recv2[pl.ds(half * 4 + 2 * c + z, 32, stride=SLOT), :]
                 wnext[there, :] = base[there, :] + (WAVE_STEP * PENALTY) * here
     sixty = pfull.at[pl.ds(0, 60)]
-    probe_all = to_a(4, (chip - kind + lax.rem(kind + 1, 16)) * 2 + core, sixty, sixty)
+    probe_all = to_a(6, (chip - kind + lax.rem(kind + 1, 16)) * 2 + core, sixty, sixty)
     probe_all.wait_recv()
     total = jnp.concatenate([pfull[pl.ds(p, 16, stride=8), :] for p in range(PB)], axis=0)
     scale = PROBE_STEP / (AA * POS * PB)
     pnext[0] = probe[0] - scale * total[:, :64]
     pnext[1] = probe[1] - scale * swap(total)[:, :64]
 
-    for copy in gathers + reduces + probe_x + ray_moves + [swap1, move1, swap2, move2, probe_all]:
+    xs = gathers + reduces[0] + reduces[1] + probe_x + ray_moves
+    for copy in xs + swaps + [move1, move2, probe_all]:
         copy.wait_send()
 
 
@@ -696,8 +716,8 @@
             vmem((CHIPS * SLOT, 128), F32),
             vmem((256, 128), F32),
             vmem((256, 128), F32),
-            vmem((128, 128), F32),
-            vmem((128, 128), F32),
+            vmem((144, 128), F32),
+            vmem((144, 128), F32),
             vmem((CHIPS * SLOT, 128), F32),
             vmem((CHIPS * SLOT, 128), F32),
             vmem((512, 256), BF16),
@@ -707,10 +727,10 @@
             vmem((64, 128), F32),
             pltpu.SemaphoreType.DMA((14,)),
             pltpu.SemaphoreType.DMA((WCH,)),
-            pltpu.SemaphoreType.DMA((12,)),
-            pltpu.SemaphoreType.DMA((12,)),
-            pltpu.SemaphoreType.DMA((5,)),
-            pltpu.SemaphoreType.DMA((5,)),
+            pltpu.SemaphoreType.DMA((15,)),
+            pltpu.SemaphoreType.DMA((15,)),
+            pltpu.SemaphoreType.DMA((7,)),
+            pltpu.SemaphoreType.DMA((7,)),
         ],
         compiler_params=pltpu.CompilerParams(
             collective_id=0, has_side_effects=True, vmem_limit_bytes=60 * 1024 * 1024

time: 41.3 us -> 39 us (0.944)
  Pallas kernels: 40.4 us -> 38.3 us
    pallas_call x1, Pallas kernels: 39.3 us -> 37.2 us  [shards(): pl.pallas_call(kernel, out_shape=(pltpu.VMEM((256, 128), F32), pltpu.VMEM...]
where the time goes in v6:
time: 39 us; the launch traced here: 38.9 us
  Pallas kernels  38.3 us (98%)
  between operations  0.64 us (2%)
    pallas_call x1, Pallas kernels, shards(): pl.pallas_call(kernel, out_shape=(pltpu.VMEM((256, 128), F32), pltpu.VMEM...  37.2 us
    pallas_call x1, Pallas kernels, shards(): pl.pallas_call(tail, out_shape=(jax.ShapeDtypeStruct((256, 128), F32), ja...  1.07 us

profile of v6, /device:TPU:1, one launch (start us, length us, event | category | flops | bytes accessed | tf_op | source)
XLA Modules:
  0.0 38.9 jit_solution(9169679905633558622)
XLA Ops:
  0.6 37.2 %admm.1 = (f32[256,128]{1,0:T(8,128)S(1)}, f32[2,64,64]{2,1,0:T(8,128)S(1)}, f32[2048,128]{1,0:T(8,128)S(1)}) custom-call(s32[1,16]{1,0:T(1,128)} %rows_ref.1, s32[1,16]{1,0:T(1,128)} %cols_ref.1, s32[1,16]{1,0:T(1,128)} %mask_ref.1, f32[512,512]{1,0:T(8,128)} %bitcast.12, bf16[4096,768]{1,0:T(8,128)(2,1)} %wts_hbm.1, f32[256,512]{1,0:T(8,128)} %bitcast.13, ...), custom_call_target="tpu_custom_call" | custom-call | tf_op jit(solution)/shard_map/admm/pallas_call | solution.py:677
  37.9 1.1 %tail.1 = (f32[256,128]{1,0:T(8,128)}, f32[2,64,64]{2,1,0:T(8,128)}, f32[512,512]{1,0:T(8,128)}) custom-call(f32[256,128]{1,0:T(8,128)S(1)} %get-tuple-element.9.wnext, f32[2,64,64]{2,1,0:T(8,128)S(1)} %get-tuple-element.10.pnext, f32[2048,128]{1,0:T(8,128)S(1)} %get-tuple-element.11.onew), custom_call_target="tpu_custom_call" | custom-call | tf_op jit(solution)/shard_map/tail/pallas_call | solution.py:753

commit v7 on v6

--- a/solution.py
+++ b/solution.py
@@ -115,6 +115,7 @@
     pnext,
     onew,
     wts,
+    wts_t,
     obj,
     wave,
     dual,
@@ -323,6 +324,20 @@
             device_id_type=pl.DeviceIdType.MESH,
         )
 
+    early = chip // 4 < 2
+
+    def turn():
+        for n in range(WCH):
+            part = slice(n * WROWS, (n + 1) * WROWS)
+            wts_t[:, part] = jnp.transpose(wts[part, :])
+
+    @pl.when(early)
+    def _():
+        for copy in wts_in:
+            copy.wait()
+        turn()
+
+    pfull[...] = jnp.zeros_like(pfull)
     pl.semaphore_wait(barrier, CHIPS + PB - 1)
     reduces = [[], []]
     for half in range(2):
@@ -372,7 +387,7 @@
     for half in range(2):
         products = jnp.zeros((64, WIDE), F32)
         for c in range(4):
-            wts_in[half * 4 + c].wait()
+            pl.when(jnp.logical_not(early))(wts_in[half * 4 + c].wait)
             part = jnp.concatenate(
                 [lhs[(c * 8 + n) * 64 : (c * 8 + n + 1) * 64, :] for n in range(8)], axis=1
             ).astype(BF16)
@@ -528,6 +543,7 @@
             probe_chip = probe_share + arrived1[64:80, :]
             message1[pl.ds(8, 32, stride=SLOT), :] = jnp.concatenate([probe_chip] * 2, axis=0)
         move1 = exchange(2, half, message1, recv1, 9)
+    pl.when(jnp.logical_not(early))(turn)
 
     for copy in gathers:
         copy.wait_recv()
@@ -580,12 +596,16 @@
     own_four = pl.ds(pl.multiple_of(kind * 8, 8), 4)
     pfull[own_four, :] = jnp.concatenate([prow[p * 8 : p * 8 + 1, :] for p in range(PB)], axis=0)
 
-    def share_rows(step):
-        four = pfull.at[own_four]
-        return to_a(6, (chip - kind + lax.rem(kind + step, 16)) * 2 + core, four, four)
-
-    for step in range(1, 16):
-        share_rows(step).start()
+    def along_y(step, rows):
+        peer = chip - chip % 4 + lax.rem(chip + step, 4)
+        return to_a(6, peer * 2 + core, rows, rows)
+
+    def along_z(step, rows):
+        peer = chip - kind + lax.rem(kind + 4 * step, 16)
+        return to_a(7, peer * 2 + core, rows, rows)
+
+    for step in range(1, 4):
+        along_y(step, pfull.at[own_four]).start()
 
     for copy in ray_moves:
         copy.wait_recv()
@@ -605,13 +625,12 @@
         [spread[t * 64 : (t + 1) * 64, :] for t in range(6)], axis=1
     ).astype(BF16)
 
+    probe_y = along_y(1, pfull.at[pl.ds(0, 12)])
+    probe_y.wait_recv()
+    for step in range(1, 4):
+        along_z(step, pfull.at[pl.ds(pl.multiple_of((kind // 4) * 32, 32), 32)]).start()
     for n in range(WCH):
-        grad = lax.dot_general(
-            table,
-            wts[n * WROWS : (n + 1) * WROWS, :],
-            (((1,), (1,)), ((), ())),
-            preferred_element_type=F32,
-        )
+        grad = dot(table, wts_t[:, n * WROWS : (n + 1) * WROWS])
         per = 32 // WCH
         for s in range(per):
             q = n * per + s
@@ -632,16 +651,15 @@
                 there = pl.ds(c * 128 + 2 * half + z, 32, stride=4)
                 here = recv2[pl.ds(half * 4 + 2 * c + z, 32, stride=SLOT), :]
                 wnext[there, :] = base[there, :] + (WAVE_STEP * PENALTY) * here
-    sixty = pfull.at[pl.ds(0, 60)]
-    probe_all = to_a(6, (chip - kind + lax.rem(kind + 1, 16)) * 2 + core, sixty, sixty)
-    probe_all.wait_recv()
+    probe_z = along_z(1, pfull.at[pl.ds(0, 96)])
+    probe_z.wait_recv()
     total = jnp.concatenate([pfull[pl.ds(p, 16, stride=8), :] for p in range(PB)], axis=0)
     scale = PROBE_STEP / (AA * POS * PB)
     pnext[0] = probe[0] - scale * total[:, :64]
     pnext[1] = probe[1] - scale * swap(total)[:, :64]
 
     xs = gathers + reduces[0] + reduces[1] + probe_x + ray_moves
-    for copy in xs + swaps + [move1, move2, probe_all]:
+    for copy in xs + swaps + [move1, move2, probe_y, probe_z]:
         copy.wait_send()
 
 
@@ -685,6 +703,7 @@
         out_specs=[vmem_spec] * 3,
         scratch_shapes=[
             vmem((4096, 768), BF16),
+            vmem((768, 4096), BF16),
             vmem((2048, 128), F32),
             vmem((1024, 128), F32),
             vmem((256, 128), F32),
@@ -729,8 +748,8 @@
             pltpu.SemaphoreType.DMA((WCH,)),
             pltpu.SemaphoreType.DMA((15,)),
             pltpu.SemaphoreType.DMA((15,)),
-            pltpu.SemaphoreType.DMA((7,)),
-            pltpu.SemaphoreType.DMA((7,)),
+            pltpu.SemaphoreType.DMA((8,)),
+            pltpu.SemaphoreType.DMA((8,)),
         ],
         compiler_params=pltpu.CompilerParams(
             collective_id=0, has_side_effects=True, vmem_limit_bytes=60 * 1024 * 1024

time: 39 us -> 40.6 us (1.041)
  Pallas kernels: 38.3 us -> 39.9 us
    pallas_call x1, Pallas kernels: 37.2 us -> 38.8 us  [shards(): pl.pallas_call(kernel, out_shape=(pltpu.VMEM((256, 128), F32), pltpu.VMEM...]
where the time goes in v7:
time: 40.6 us; the launch traced here: 40.5 us
  Pallas kernels  39.9 us (98%)
  between operations  0.64 us (2%)
    pallas_call x1, Pallas kernels, shards(): pl.pallas_call(kernel, out_shape=(pltpu.VMEM((256, 128), F32), pltpu.VMEM...  38.8 us
    pallas_call x1, Pallas kernels, shards(): pl.pallas_call(tail, out_shape=(jax.ShapeDtypeStruct((256, 128), F32), ja...  1.07 us

profile of v7, /device:TPU:1, one launch (start us, length us, event | category | flops | bytes accessed | tf_op | source)
XLA Modules:
  0.0 40.5 jit_solution(9046399342500564854)
XLA Ops:
  0.6 38.8 %admm.1 = (f32[256,128]{1,0:T(8,128)S(1)}, f32[2,64,64]{2,1,0:T(8,128)S(1)}, f32[2048,128]{1,0:T(8,128)S(1)}) custom-call(s32[1,16]{1,0:T(1,128)} %rows_ref.1, s32[1,16]{1,0:T(1,128)} %cols_ref.1, s32[1,16]{1,0:T(1,128)} %mask_ref.1, f32[512,512]{1,0:T(8,128)} %bitcast.12, bf16[4096,768]{1,0:T(8,128)(2,1)} %wts_hbm.1, f32[256,512]{1,0:T(8,128)} %bitcast.13, ...), custom_call_target="tpu_custom_call" | custom-call | tf_op jit(solution)/shard_map/admm/pallas_call | solution.py:695
  39.4 1.1 %tail.1 = (f32[256,128]{1,0:T(8,128)}, f32[2,64,64]{2,1,0:T(8,128)}, f32[512,512]{1,0:T(8,128)}) custom-call(f32[256,128]{1,0:T(8,128)S(1)} %get-tuple-element.9.wnext, f32[2,64,64]{2,1,0:T(8,128)S(1)} %get-tuple-element.10.pnext, f32[2048,128]{1,0:T(8,128)S(1)} %get-tuple-element.11.onew), custom_call_target="tpu_custom_call" | custom-call | tf_op jit(solution)/shard_map/tail/pallas_call | solution.py:772

commit v8 on v7

--- a/solution.py
+++ b/solution.py
@@ -324,18 +324,16 @@
             device_id_type=pl.DeviceIdType.MESH,
         )
 
-    early = chip // 4 < 2
-
-    def turn():
-        for n in range(WCH):
-            part = slice(n * WROWS, (n + 1) * WROWS)
-            wts_t[:, part] = jnp.transpose(wts[part, :])
+    early = chip // 4 == 0
+    late = chip // 16 == 1
 
     @pl.when(early)
     def _():
         for copy in wts_in:
             copy.wait()
-        turn()
+        for n in range(WCH):
+            part = slice(n * WROWS, (n + 1) * WROWS)
+            wts_t[:, part] = jnp.transpose(wts[part, :])
 
     pfull[...] = jnp.zeros_like(pfull)
     pl.semaphore_wait(barrier, CHIPS + PB - 1)
@@ -543,7 +541,6 @@
             probe_chip = probe_share + arrived1[64:80, :]
             message1[pl.ds(8, 32, stride=SLOT), :] = jnp.concatenate([probe_chip] * 2, axis=0)
         move1 = exchange(2, half, message1, recv1, 9)
-    pl.when(jnp.logical_not(early))(turn)
 
     for copy in gathers:
         copy.wait_recv()
@@ -560,6 +557,10 @@
         later[half].wait_recv()
         fill(half, loose2, arrived2, message2)
     swaps += later
+
+    @pl.when(late)
+    def _():
+        exchange(5, 0, message2, recv2, 8)
 
     move1.wait_recv()
     for half in range(2):
@@ -587,8 +588,11 @@
     for copy in probe_x:
         copy.start()
 
-    for half in range(2):
-        move2 = exchange(5, half, message2, recv2, 8)
+    @pl.when(jnp.logical_not(late))
+    def _():
+        exchange(5, 0, message2, recv2, 8)
+
+    move2 = exchange(5, 1, message2, recv2, 8)
 
     for copy in probe_x:
         copy.wait_recv()
@@ -629,20 +633,33 @@
     probe_y.wait_recv()
     for step in range(1, 4):
         along_z(step, pfull.at[pl.ds(pl.multiple_of((kind // 4) * 32, 32), 32)]).start()
-    for n in range(WCH):
-        grad = dot(table, wts_t[:, n * WROWS : (n + 1) * WROWS])
+    def object_step(product):
         per = 32 // WCH
-        for s in range(per):
-            q = n * per + s
-            for t in range(4):
-                first, second = interleave(
-                    grad[t * 16 : t * 16 + 8, s * 128 : (s + 1) * 128],
-                    grad[t * 16 + 8 : t * 16 + 16, s * 128 : (s + 1) * 128],
-                )
-                even = pl.ds(t * 512 + 2 * q, 8, stride=64)
-                odd = pl.ds(t * 512 + 2 * q + 1, 8, stride=64)
-                onew[even, :] = obj[even, :] - OBJECT_STEP * first
-                onew[odd, :] = obj[odd, :] - OBJECT_STEP * second
+        for n in range(WCH):
+            grad = product(slice(n * WROWS, (n + 1) * WROWS))
+            for s in range(per):
+                q = n * per + s
+                for t in range(4):
+                    first, second = interleave(
+                        grad[t * 16 : t * 16 + 8, s * 128 : (s + 1) * 128],
+                        grad[t * 16 + 8 : t * 16 + 16, s * 128 : (s + 1) * 128],
+                    )
+                    even = pl.ds(t * 512 + 2 * q, 8, stride=64)
+                    odd = pl.ds(t * 512 + 2 * q + 1, 8, stride=64)
+                    onew[even, :] = obj[even, :] - OBJECT_STEP * first
+                    onew[odd, :] = obj[odd, :] - OBJECT_STEP * second
+
+    @pl.when(early)
+    def _():
+        object_step(lambda part: dot(table, wts_t[:, part]))
+
+    @pl.when(jnp.logical_not(early))
+    def _():
+        object_step(
+            lambda part: lax.dot_general(
+                table, wts[part, :], (((1,), (1,)), ((), ())), preferred_element_type=F32
+            )
+        )
 
     move2.wait_recv()
     for half in range(2):

time: 40.6 us -> 40.6 us (level)
  no operation moved by 1% of the time
where the time goes in v8:
time: 40.6 us; the launch traced here: 40.2 us
  Pallas kernels  39.6 us (98%)
  between operations  0.64 us (2%)
    pallas_call x1, Pallas kernels, shards(): pl.pallas_call(kernel, out_shape=(pltpu.VMEM((256, 128), F32), pltpu.VMEM...  38.5 us
    pallas_call x1, Pallas kernels, shards(): pl.pallas_call(tail, out_shape=(jax.ShapeDtypeStruct((256, 128), F32), ja...  1.07 us

profile of v8, /device:TPU:1, one launch (start us, length us, event | category | flops | bytes accessed | tf_op | source)
XLA Modules:
  0.0 40.2 jit_solution(13532623100500331468)
XLA Ops:
  0.6 38.5 %admm.1 = (f32[256,128]{1,0:T(8,128)S(1)}, f32[2,64,64]{2,1,0:T(8,128)S(1)}, f32[2048,128]{1,0:T(8,128)S(1)}) custom-call(s32[1,16]{1,0:T(1,128)} %rows_ref.1, s32[1,16]{1,0:T(1,128)} %cols_ref.1, s32[1,16]{1,0:T(1,128)} %mask_ref.1, f32[512,512]{1,0:T(8,128)} %bitcast.12, bf16[4096,768]{1,0:T(8,128)(2,1)} %wts_hbm.1, f32[256,512]{1,0:T(8,128)} %bitcast.13, ...), custom_call_target="tpu_custom_call" | custom-call | tf_op jit(solution)/shard_map/admm/pallas_call | solution.py:712
  39.1 1.1 %tail.1 = (f32[256,128]{1,0:T(8,128)}, f32[2,64,64]{2,1,0:T(8,128)}, f32[512,512]{1,0:T(8,128)}) custom-call(f32[256,128]{1,0:T(8,128)S(1)} %get-tuple-element.9.wnext, f32[2,64,64]{2,1,0:T(8,128)S(1)} %get-tuple-element.10.pnext, f32[2048,128]{1,0:T(8,128)S(1)} %get-tuple-element.11.onew), custom_call_target="tpu_custom_call" | custom-call | tf_op jit(solution)/shard_map/tail/pallas_call | solution.py:789

commit v9 on v8

--- a/solution.py
+++ b/solution.py
@@ -335,7 +335,6 @@
             part = slice(n * WROWS, (n + 1) * WROWS)
             wts_t[:, part] = jnp.transpose(wts[part, :])
 
-    pfull[...] = jnp.zeros_like(pfull)
     pl.semaphore_wait(barrier, CHIPS + PB - 1)
     reduces = [[], []]
     for half in range(2):
@@ -600,16 +599,12 @@
     own_four = pl.ds(pl.multiple_of(kind * 8, 8), 4)
     pfull[own_four, :] = jnp.concatenate([prow[p * 8 : p * 8 + 1, :] for p in range(PB)], axis=0)
 
-    def along_y(step, rows):
-        peer = chip - chip % 4 + lax.rem(chip + step, 4)
+    def share_rows(step, rows):
+        peer = chip - kind + lax.rem(kind + step, 16)
         return to_a(6, peer * 2 + core, rows, rows)
 
-    def along_z(step, rows):
-        peer = chip - kind + lax.rem(kind + 4 * step, 16)
-        return to_a(7, peer * 2 + core, rows, rows)
-
-    for step in range(1, 4):
-        along_y(step, pfull.at[own_four]).start()
+    for step in range(1, 16):
+        share_rows(step, pfull.at[own_four]).start()
 
     for copy in ray_moves:
         copy.wait_recv()
@@ -629,10 +624,6 @@
         [spread[t * 64 : (t + 1) * 64, :] for t in range(6)], axis=1
     ).astype(BF16)
 
-    probe_y = along_y(1, pfull.at[pl.ds(0, 12)])
-    probe_y.wait_recv()
-    for step in range(1, 4):
-        along_z(step, pfull.at[pl.ds(pl.multiple_of((kind // 4) * 32, 32), 32)]).start()
     def object_step(product):
         per = 32 // WCH
         for n in range(WCH):
@@ -668,15 +659,15 @@
                 there = pl.ds(c * 128 + 2 * half + z, 32, stride=4)
                 here = recv2[pl.ds(half * 4 + 2 * c + z, 32, stride=SLOT), :]
                 wnext[there, :] = base[there, :] + (WAVE_STEP * PENALTY) * here
-    probe_z = along_z(1, pfull.at[pl.ds(0, 96)])
-    probe_z.wait_recv()
+    probe_all = share_rows(1, pfull.at[pl.ds(0, 60)])
+    probe_all.wait_recv()
     total = jnp.concatenate([pfull[pl.ds(p, 16, stride=8), :] for p in range(PB)], axis=0)
     scale = PROBE_STEP / (AA * POS * PB)
     pnext[0] = probe[0] - scale * total[:, :64]
     pnext[1] = probe[1] - scale * swap(total)[:, :64]
 
     xs = gathers + reduces[0] + reduces[1] + probe_x + ray_moves
-    for copy in xs + swaps + [move1, move2, probe_y, probe_z]:
+    for copy in xs + swaps + [move1, move2, probe_all]:
         copy.wait_send()
 
 
@@ -765,8 +756,8 @@
             pltpu.SemaphoreType.DMA((WCH,)),
             pltpu.SemaphoreType.DMA((15,)),
             pltpu.SemaphoreType.DMA((15,)),
-            pltpu.SemaphoreType.DMA((8,)),
-            pltpu.SemaphoreType.DMA((8,)),
+            pltpu.SemaphoreType.DMA((7,)),
+            pltpu.SemaphoreType.DMA((7,)),
         ],
         compiler_params=pltpu.CompilerParams(
             collective_id=0, has_side_effects=True, vmem_limit_bytes=60 * 1024 * 1024

time: 40.6 us -> 38.9 us (0.958)
  Pallas kernels: 39.6 us -> 38.2 us
    pallas_call x1, Pallas kernels: 38.5 us -> 37.1 us  [shards(): pl.pallas_call(kernel, out_shape=(pltpu.VMEM((256, 128), F32), pltpu.VMEM...]
where the time goes in v9:
time: 38.9 us; the launch traced here: 38.8 us
  Pallas kernels  38.2 us (98%)
  between operations  0.64 us (2%)
    pallas_call x1, Pallas kernels, shards(): pl.pallas_call(kernel, out_shape=(pltpu.VMEM((256, 128), F32), pltpu.VMEM...  37.1 us
    pallas_call x1, Pallas kernels, shards(): pl.pallas_call(tail, out_shape=(jax.ShapeDtypeStruct((256, 128), F32), ja...  1.07 us

profile of v9, /device:TPU:1, one launch (start us, length us, event | category | flops | bytes accessed | tf_op | source)
XLA Modules:
  0.0 38.8 jit_solution(12575647447824049698)
XLA Ops:
  0.6 37.1 %admm.1 = (f32[256,128]{1,0:T(8,128)S(1)}, f32[2,64,64]{2,1,0:T(8,128)S(1)}, f32[2048,128]{1,0:T(8,128)S(1)}) custom-call(s32[1,16]{1,0:T(1,128)} %rows_ref.1, s32[1,16]{1,0:T(1,128)} %cols_ref.1, s32[1,16]{1,0:T(1,128)} %mask_ref.1, f32[512,512]{1,0:T(8,128)} %bitcast.12, bf16[4096,768]{1,0:T(8,128)(2,1)} %wts_hbm.1, f32[256,512]{1,0:T(8,128)} %bitcast.13, ...), custom_call_target="tpu_custom_call" | custom-call | tf_op jit(solution)/shard_map/admm/pallas_call | solution.py:703
  37.8 1.1 %tail.1 = (f32[256,128]{1,0:T(8,128)}, f32[2,64,64]{2,1,0:T(8,128)}, f32[512,512]{1,0:T(8,128)}) custom-call(f32[256,128]{1,0:T(8,128)S(1)} %get-tuple-element.9.wnext, f32[2,64,64]{2,1,0:T(8,128)S(1)} %get-tuple-element.10.pnext, f32[2048,128]{1,0:T(8,128)S(1)} %get-tuple-element.11.onew), custom_call_target="tpu_custom_call" | custom-call | tf_op jit(solution)/shard_map/tail/pallas_call | solution.py:780

commit v10 on v9

--- a/solution.py
+++ b/solution.py
@@ -582,10 +582,13 @@
         copy.start()
 
     own_row = pl.ds(pl.multiple_of(me_p * 8, 8), 1)
-    prow[own_row, :] = jnp.sum(recv1[pl.ds(8, 32, stride=SLOT), :], axis=0, keepdims=True)
     probe_x = [to_x(4, step, prow.at[own_row], prow.at[own_row]) for step in (2, 1, 3)]
-    for copy in probe_x:
-        copy.start()
+
+    @pl.when(late)
+    def _():
+        prow[own_row, :] = jnp.sum(recv1[pl.ds(8, 32, stride=SLOT), :], axis=0, keepdims=True)
+        for copy in probe_x:
+            copy.start()
 
     @pl.when(jnp.logical_not(late))
     def _():
@@ -593,18 +596,23 @@
 
     move2 = exchange(5, 1, message2, recv2, 8)
 
-    for copy in probe_x:
-        copy.wait_recv()
     kind = chip % 16
     own_four = pl.ds(pl.multiple_of(kind * 8, 8), 4)
-    pfull[own_four, :] = jnp.concatenate([prow[p * 8 : p * 8 + 1, :] for p in range(PB)], axis=0)
-
-    def share_rows(step, rows):
-        peer = chip - kind + lax.rem(kind + step, 16)
-        return to_a(6, peer * 2 + core, rows, rows)
-
-    for step in range(1, 16):
-        share_rows(step, pfull.at[own_four]).start()
+
+    def share_rows(first, step, rows):
+        return to_a(6, (first + lax.rem(kind + step, 16)) * 2 + core, rows, rows)
+
+    @pl.when(late)
+    def _():
+        for copy in probe_x:
+            copy.wait_recv()
+        pfull[own_four, :] = jnp.concatenate(
+            [prow[p * 8 : p * 8 + 1, :] for p in range(PB)], axis=0
+        )
+        for step in range(16):
+            share_rows(0, step, pfull.at[own_four]).start()
+        for step in range(1, 16):
+            share_rows(16, step, pfull.at[own_four]).start()
 
     for copy in ray_moves:
         copy.wait_recv()
@@ -659,15 +667,27 @@
                 there = pl.ds(c * 128 + 2 * half + z, 32, stride=4)
                 here = recv2[pl.ds(half * 4 + 2 * c + z, 32, stride=SLOT), :]
                 wnext[there, :] = base[there, :] + (WAVE_STEP * PENALTY) * here
-    probe_all = share_rows(1, pfull.at[pl.ds(0, 60)])
-    probe_all.wait_recv()
+    @pl.when(late)
+    def _():
+        rows = pfull.at[pl.ds(0, 60)]
+        share_rows(16, 1, rows).wait_recv()
+        rows = pfull.at[pl.ds(0, 124)]
+        share_rows(16, 1, rows).wait_send()
+        for copy in probe_x:
+            copy.wait_send()
+
+    @pl.when(jnp.logical_not(late))
+    def _():
+        rows = pfull.at[pl.ds(0, 64)]
+        to_a(6, (16 + kind) * 2 + core, rows, rows).wait_recv()
+
     total = jnp.concatenate([pfull[pl.ds(p, 16, stride=8), :] for p in range(PB)], axis=0)
     scale = PROBE_STEP / (AA * POS * PB)
     pnext[0] = probe[0] - scale * total[:, :64]
     pnext[1] = probe[1] - scale * swap(total)[:, :64]
 
-    xs = gathers + reduces[0] + reduces[1] + probe_x + ray_moves
-    for copy in xs + swaps + [move1, move2, probe_all]:
+    xs = gathers + reduces[0] + reduces[1] + ray_moves
+    for copy in xs + swaps + [move1, move2]:
         copy.wait_send()
 
 

time: 38.9 us -> 42.6 us (1.095)
  Pallas kernels: 38.2 us -> 41.9 us
    pallas_call x1, Pallas kernels: 37.1 us -> 40.8 us  [shards(): pl.pallas_call(kernel, out_shape=(pltpu.VMEM((256, 128), F32), pltpu.VMEM...]
where the time goes in v10:
time: 42.6 us; the launch traced here: 42.5 us
  Pallas kernels  41.9 us (98%)
  between operations  0.64 us (2%)
    pallas_call x1, Pallas kernels, shards(): pl.pallas_call(kernel, out_shape=(pltpu.VMEM((256, 128), F32), pltpu.VMEM...  40.8 us
    pallas_call x1, Pallas kernels, shards(): pl.pallas_call(tail, out_shape=(jax.ShapeDtypeStruct((256, 128), F32), ja...  1.07 us

profile of v10, /device:TPU:1, one launch (start us, length us, event | category | flops | bytes accessed | tf_op | source)
XLA Modules:
  0.0 42.5 jit_solution(11837170399367544620)
XLA Ops:
  0.6 40.8 %admm.1 = (f32[256,128]{1,0:T(8,128)S(1)}, f32[2,64,64]{2,1,0:T(8,128)S(1)}, f32[2048,128]{1,0:T(8,128)S(1)}) custom-call(s32[1,16]{1,0:T(1,128)} %rows_ref.1, s32[1,16]{1,0:T(1,128)} %cols_ref.1, s32[1,16]{1,0:T(1,128)} %mask_ref.1, f32[512,512]{1,0:T(8,128)} %bitcast.12, bf16[4096,768]{1,0:T(8,128)(2,1)} %wts_hbm.1, f32[256,512]{1,0:T(8,128)} %bitcast.13, ...), custom_call_target="tpu_custom_call" | custom-call | tf_op jit(solution)/shard_map/admm/pallas_call | solution.py:723
  41.4 1.1 %tail.1 = (f32[256,128]{1,0:T(8,128)}, f32[2,64,64]{2,1,0:T(8,128)}, f32[512,512]{1,0:T(8,128)}) custom-call(f32[256,128]{1,0:T(8,128)S(1)} %get-tuple-element.9.wnext, f32[2,64,64]{2,1,0:T(8,128)S(1)} %get-tuple-element.10.pnext, f32[2048,128]{1,0:T(8,128)S(1)} %get-tuple-element.11.onew), custom_call_target="tpu_custom_call" | custom-call | tf_op jit(solution)/shard_map/tail/pallas_call | solution.py:800
